TPU v7x, 32 devices: a whole 2x2x4 slice. The times are simulated.
32 devices in a mesh: dp: 4 (over x, core), fsdp: 8 (over z, y).
Axes of the slice: x: 2, y: 2, z: 4, core: 2. Of those that a mesh axis runs over, the one named last changes fastest.
Arguments:
- tokens: bfloat16 [32, 256, 1024], P(('dp', 'fsdp')), may hold values from -6 to 6
- memory: bfloat16 [32, 256, 1024], P(('dp', 'fsdp')), may hold values from -6 to 6
- token_segments: int32 [32, 256], P(('dp', 'fsdp')), may hold values from 0 to 3, never falling along the last dimension, each value on 1 to 128 neighbouring positions
- memory_segments: int32 [32, 256], P(('dp', 'fsdp')), may hold values from 0 to 3, never falling along the last dimension, each value on 1 to 128 neighbouring positions
- padding: int32 [32, 256], P(('dp', 'fsdp')), may hold values 0 or 1
- self_project: bfloat16 [3, 1024, 1024], P(None, ('dp', 'fsdp')), may hold values from -0.1875 to 0.1875
- self_output: bfloat16 [1024, 1024], P(('dp', 'fsdp')), may hold values from -0.75 to 0.75
- cross_project: bfloat16 [3, 1024, 1024], P(None, ('dp', 'fsdp')), may hold values from -0.1875 to 0.1875
- cross_output: bfloat16 [1024, 1024], P(('dp', 'fsdp')), may hold values from -0.75 to 0.75
- widen_weight: bfloat16 [1024, 4096], P(('dp', 'fsdp')), may hold values from -0.1875 to 0.1875
- narrow_weight: bfloat16 [4096, 1024], P(('dp', 'fsdp')), may hold values from -0.1875 to 0.1875
- norm_gain: bfloat16 [3, 1024], P(None, ('dp', 'fsdp')), may hold values from 0.5 to 1.5
- norm_bias: bfloat16 [3, 1024], P(None, ('dp', 'fsdp')), may hold values from -2 to 2
- grad_out: bfloat16 [32, 256, 1024], P(('dp', 'fsdp')), may hold values from -6 to 6
Outputs:
- layer_out: bfloat16 [32, 256, 1024], P(('dp', 'fsdp'))
- grad_tokens: float32 [32, 256, 1024], P(('dp', 'fsdp'))
- grad_memory: float32 [32, 256, 1024], P(('dp', 'fsdp'))
- grad_self_project: float32 [3, 1024, 1024], P(None, ('dp', 'fsdp'))
- grad_self_output: float32 [1024, 1024], P(('dp', 'fsdp'))
- grad_cross_project: float32 [3, 1024, 1024], P(None, ('dp', 'fsdp'))
- grad_cross_output: float32 [1024, 1024], P(('dp', 'fsdp'))
- grad_widen: float32 [1024, 4096], P(('dp', 'fsdp'))
- grad_narrow: float32 [4096, 1024], P(('dp', 'fsdp'))
- grad_norm_gain: float32 [3, 1024], P(None, ('dp', 'fsdp'))
- grad_norm_bias: float32 [3, 1024], P(None, ('dp', 'fsdp'))
Inputs may be any that keep to these rules, and one draw needn't show every extreme that they name: `token_segments`: each row holds all 4 segments in order, one of them 256 // 2 tokens long. `memory_segments`: each row holds all 4 segments in order, one of them 256 // 2 tokens long.
All inputs are finite; a program needn't handle non-finite values. No bound on the sum of `padding` on one device may be relied on, other than what follows from the above.
Results may differ from a plain program's by a relative error of at most 0.013.
Values may be sent and summed in bfloat16 or wider, within the bound.
No kernel may reach another device: no remote copies, remote signals or barrier semaphores. Data moves between devices by JAX's collectives and lax.ppermute only.
A program may use at most 256 MiB of HBM per device.

v0:
```python
import jax
import jax.numpy as jnp
from jax import lax
from jax.sharding import PartitionSpec as P

HEADS = 16
HEAD = 64


ALPHA = (3.0 * 200.0) ** 0.25
EPSILON = 1e-05
MASKED = -1e30


def rounded(values_in):
    return values_in.astype(jnp.bfloat16)


def product(first_side, other_side):
    return jnp.dot(first_side, other_side, preferred_element_type=jnp.float32)


def normalize(values_in, scale_row, shift_row):
    average = jnp.mean(values_in, axis=-1, keepdims=True)
    centred = values_in - average
    spread = jnp.mean(centred * centred, axis=-1, keepdims=True)
    return centred * lax.rsqrt(spread + EPSILON) * scale_row + shift_row


def normalize_back(values_in, scale_row, shift_row, grad_result):
    unused, pullback = jax.vjp(normalize, values_in, scale_row, shift_row)
    return pullback(grad_result)


def project_three(query_source, key_source, weight_stack):
    return (
        rounded(product(query_source, weight_stack[0])),
        rounded(product(key_source, weight_stack[1])),
        rounded(product(key_source, weight_stack[2])),
    )


def project_inputs(weight_stack, grad_query, grad_key, grad_value):
    grad_query_side = product(grad_query, weight_stack[0].T)
    grad_key_side = product(grad_key, weight_stack[1].T) + product(grad_value, weight_stack[2].T)
    return (grad_query_side, grad_key_side)


def split_terms(terms, width):
    stack_rows = terms[:, : 3 * width].reshape(terms.shape[0], 3, width).transpose(1, 0, 2)
    return (stack_rows, terms[:, 3 * width :])


def masked_scores(head_query, head_key, allowed):
    scores = jnp.einsum(
        "qhd,khd->hqk", head_query, head_key, preferred_element_type=jnp.float32
    ) * HEAD ** (-0.5)
    return jnp.where(allowed[None], scores, MASKED)


def attend_forward(queries, key_rows, values, allowed):
    length = queries.shape[0]
    key_count = key_rows.shape[0]
    head_query = queries.reshape(length, HEADS, HEAD)
    head_key = key_rows.reshape(key_count, HEADS, HEAD)
    head_value = values.reshape(key_count, HEADS, HEAD)
    scores = masked_scores(head_query, head_key, allowed)
    largest = jnp.max(scores, axis=-1, keepdims=True)
    exponentials = jnp.exp(scores - largest)
    totals = jnp.sum(exponentials, axis=-1, keepdims=True)
    weights = rounded(exponentials / totals)
    mixed = jnp.einsum("hqk,khd->qhd", weights, head_value, preferred_element_type=jnp.float32)
    return (rounded(mixed.reshape(length, HEADS * HEAD)), largest + jnp.log(totals))


def attend_backward(queries, key_rows, values, allowed, logsum, grad_mixed):
    length = queries.shape[0]
    key_count = key_rows.shape[0]
    head_query = queries.reshape(length, HEADS, HEAD)
    head_key = key_rows.reshape(key_count, HEADS, HEAD)
    head_value = values.reshape(key_count, HEADS, HEAD)
    head_grad = grad_mixed.reshape(length, HEADS, HEAD)
    weights = jnp.exp(masked_scores(head_query, head_key, allowed) - logsum)
    grad_values = jnp.einsum(
        "hqk,qhd->khd", rounded(weights), head_grad, preferred_element_type=jnp.float32
    )
    grad_weights = jnp.einsum(
        "qhd,khd->hqk", head_grad, head_value, preferred_element_type=jnp.float32
    )
    inner_sum = jnp.sum(weights * grad_weights, axis=-1, keepdims=True)
    grad_scores = rounded(weights * (grad_weights - inner_sum))
    grad_queries = jnp.einsum(
        "hqk,khd->qhd", grad_scores, head_key, preferred_element_type=jnp.float32
    ) * HEAD ** (-0.5)
    grad_keys = jnp.einsum(
        "hqk,qhd->khd", grad_scores, head_query, preferred_element_type=jnp.float32
    ) * HEAD ** (-0.5)
    return (
        rounded(grad_queries.reshape(length, HEADS * HEAD)),
        rounded(grad_keys.reshape(key_count, HEADS * HEAD)),
        rounded(grad_values.reshape(key_count, HEADS * HEAD)),
    )


def per_device(
    tokens,
    memory,
    token_segments,
    memory_segments,
    padding,
    self_project,
    self_output,
    cross_project,
    cross_output,
    widen_weight,
    narrow_weight,
    norm_gain,
    norm_bias,
    grad_out,
):
    token_low = tokens[0]
    memory_low = memory[0]
    row_in = token_low.astype(jnp.float32)
    segment_row = token_segments[0]
    places = jnp.arange(segment_row.shape[0])
    diagonal = places[None, :] == places[:, None]
    live_keys = padding[0] == 1
    self_allowed = (
        (segment_row[:, None] == segment_row[None, :])
        & (places[None, :] <= places[:, None])
        & (live_keys[None, :] | diagonal)
    )
    cross_allowed = segment_row[:, None] == memory_segments[0][None, :]
    pad_scale = padding[0].astype(jnp.float32)[:, None]
    width = token_low.shape[1]
    self_stack, self_final, gain_rows, bias_rows = (
        lax.all_gather(self_project, ("dp", "fsdp"), axis=1, tiled=True),
        lax.all_gather(self_output, ("dp", "fsdp"), axis=0, tiled=True),
        lax.all_gather(norm_gain, ("dp", "fsdp"), axis=1, tiled=True),
        lax.all_gather(norm_bias, ("dp", "fsdp"), axis=1, tiled=True),
    )
    gain_values = gain_rows.astype(jnp.float32)
    bias_values = bias_rows.astype(jnp.float32)
    self_query, self_key, self_value = project_three(token_low, token_low, self_stack)
    self_mixed, self_logsum = attend_forward(self_query, self_key, self_value, self_allowed)
    pre_one = ALPHA * row_in + product(self_mixed, self_final)
    first_out = normalize(pre_one, gain_values[0], bias_values[0])
    first_low = rounded(first_out)
    cross_stack, cross_final = (
        lax.all_gather(cross_project, ("dp", "fsdp"), axis=1, tiled=True),
        lax.all_gather(cross_output, ("dp", "fsdp"), axis=0, tiled=True),
    )
    cross_query, cross_key, cross_value = project_three(first_low, memory_low, cross_stack)
    cross_mixed, cross_logsum = attend_forward(cross_query, cross_key, cross_value, cross_allowed)
    pre_two = ALPHA * first_out + product(cross_mixed, cross_final)
    second = normalize(pre_two, gain_values[1], bias_values[1])
    second_low = rounded(second)
    widen_full, narrow_full = (
        lax.all_gather(widen_weight, ("dp", "fsdp"), axis=0, tiled=True),
        lax.all_gather(narrow_weight, ("dp", "fsdp"), axis=0, tiled=True),
    )
    hidden = product(second_low, widen_full)
    active = rounded(jax.nn.gelu(hidden))
    pre_three = ALPHA * second + product(active, narrow_full)
    third_out = normalize(pre_three, gain_values[2], bias_values[2])
    layer_out = rounded(third_out * pad_scale)
    grad_third = grad_out[0].astype(jnp.float32) * pad_scale
    grad_pre_three, grad_gain_three, grad_bias_three = normalize_back(
        pre_three, gain_values[2], bias_values[2], grad_third
    )
    ffn_branch = rounded(grad_pre_three)
    grad_active = product(ffn_branch, narrow_full.T)
    unused, gelu_pull = jax.vjp(jax.nn.gelu, hidden)
    grad_hidden = rounded(gelu_pull(grad_active)[0])
    grad_second = ALPHA * grad_pre_three + product(grad_hidden, widen_full.T)
    grad_narrow = lax.psum_scatter(
        product(active.T, ffn_branch), ("dp", "fsdp"), scatter_dimension=0, tiled=True
    )
    grad_widen = lax.psum_scatter(
        product(second_low.T, grad_hidden), ("dp", "fsdp"), scatter_dimension=0, tiled=True
    )
    cross_stack, cross_final = (
        lax.all_gather(cross_project, ("dp", "fsdp"), axis=1, tiled=True),
        lax.all_gather(cross_output, ("dp", "fsdp"), axis=0, tiled=True),
    )
    cross_query, cross_key, cross_value = project_three(first_low, memory_low, cross_stack)
    grad_pre_two, grad_gain_two, grad_bias_two = normalize_back(
        pre_two, gain_values[1], bias_values[1], grad_second
    )
    cross_branch = rounded(grad_pre_two)
    grad_mixed = rounded(product(cross_branch, cross_final.T))
    cross_dq, cross_dk, cross_dv = attend_backward(
        cross_query, cross_key, cross_value, cross_allowed, cross_logsum, grad_mixed
    )
    grad_first_in, grad_memory = project_inputs(cross_stack, cross_dq, cross_dk, cross_dv)
    grad_first = ALPHA * grad_pre_two + grad_first_in
    cross_key_grads = jnp.concatenate([cross_dk, cross_dv], axis=1)
    query_part = product(first_low.T, cross_dq)
    memory_part = product(memory_low.T, cross_key_grads)
    final_part = product(cross_mixed.T, cross_branch)
    cross_rows = lax.psum_scatter(
        jnp.concatenate([query_part, memory_part, final_part], axis=1),
        ("dp", "fsdp"),
        scatter_dimension=0,
        tiled=True,
    )
    grad_cross_stack, grad_cross_final = split_terms(cross_rows, width)
    self_stack, self_final = (
        lax.all_gather(self_project, ("dp", "fsdp"), axis=1, tiled=True),
        lax.all_gather(self_output, ("dp", "fsdp"), axis=0, tiled=True),
    )
    self_query, self_key, self_value = project_three(token_low, token_low, self_stack)
    grad_pre_one, grad_gain_one, grad_bias_one = normalize_back(
        pre_one, gain_values[0], bias_values[0], grad_first
    )
    self_branch = rounded(grad_pre_one)
    grad_mixed = rounded(product(self_branch, self_final.T))
    self_dq, self_dk, self_dv = attend_backward(
        self_query, self_key, self_value, self_allowed, self_logsum, grad_mixed
    )
    grad_query_in, grad_key_in = project_inputs(self_stack, self_dq, self_dk, self_dv)
    grad_tokens = ALPHA * grad_pre_one + grad_query_in + grad_key_in
    grad_gains = jnp.stack([grad_gain_one, grad_gain_two, grad_gain_three])
    grad_biases = jnp.stack([grad_bias_one, grad_bias_two, grad_bias_three])
    self_all_grads = jnp.concatenate([self_dq, self_dk, self_dv], axis=1)
    input_part = product(token_low.T, self_all_grads)
    final_part = product(self_mixed.T, self_branch)
    self_rows = lax.psum_scatter(
        jnp.concatenate([input_part, final_part], axis=1),
        ("dp", "fsdp"),
        scatter_dimension=0,
        tiled=True,
    )
    grad_self_stack, grad_self_final = split_terms(self_rows, width)
    grad_gains, grad_biases = (
        lax.psum_scatter(grad_gains, ("dp", "fsdp"), scatter_dimension=1, tiled=True),
        lax.psum_scatter(grad_biases, ("dp", "fsdp"), scatter_dimension=1, tiled=True),
    )
    return (
        layer_out[None],
        grad_tokens[None],
        grad_memory[None],
        grad_self_stack,
        grad_self_final,
        grad_cross_stack,
        grad_cross_final,
        grad_widen,
        grad_narrow,
        grad_gains,
        grad_biases,
    )


def solution(mesh):
    return jax.shard_map(
        per_device,
        mesh=mesh,
        in_specs=(
            P(("dp", "fsdp"), None, None),
            P(("dp", "fsdp"), None, None),
            P(("dp", "fsdp"), None),
            P(("dp", "fsdp"), None),
            P(("dp", "fsdp"), None),
            P(None, ("dp", "fsdp"), None),
            P(("dp", "fsdp"), None),
            P(None, ("dp", "fsdp"), None),
            P(("dp", "fsdp"), None),
            P(("dp", "fsdp"), None),
            P(("dp", "fsdp"), None),
            P(None, ("dp", "fsdp")),
            P(None, ("dp", "fsdp")),
            P(("dp", "fsdp"), None, None),
        ),
        out_specs=(
            P(("dp", "fsdp"), None, None),
            P(("dp", "fsdp"), None, None),
            P(("dp", "fsdp"), None, None),
            P(None, ("dp", "fsdp"), None),
            P(("dp", "fsdp"), None),
            P(None, ("dp", "fsdp"), None),
            P(("dp", "fsdp"), None),
            P(("dp", "fsdp"), None),
            P(("dp", "fsdp"), None),
            P(None, ("dp", "fsdp")),
            P(None, ("dp", "fsdp")),
        ),
        check_vma=False,
    )
```

profile of v0, /device:TPU:0, one launch (start us, length us, event | category | flops | bytes accessed | tf_op | source)
XLA Modules:
  0.0 2181.8 jit_solution(17055692153350252273)
XLA Ops:
  11.9 70.4 %all-gather = bf16[32,32,3]{1,2,0:T(4,128)(2,1)S(1)} all-gather(bf16[1,32,3]{1,2,0:T(4,128)(2,1)} %bitcast.267), channel_id=1, replica_groups=mesh['dp'=4,'fsdp'=8] {'dp','fsdp'}, dimensions={0}, use_global_device_ids=true | all-gather | bytes 6336 | tf_op jit(solution)/shard_map/all_gather | solution.py:139
  82.4 63.9 %all-gather.1 = bf16[32,32,3]{1,2,0:T(4,128)(2,1)S(1)} all-gather(bf16[1,32,3]{1,2,0:T(4,128)(2,1)} %bitcast.268), channel_id=1, replica_groups=mesh['dp'=4,'fsdp'=8] {'dp','fsdp'}, dimensions={0}, use_global_device_ids=true | all-gather | bytes 6336 | tf_op jit(solution)/shard_map/all_gather | solution.py:140
  150.7 2.5 fusion.51
  159.4 2.5 fusion.54
  166.6 46.1 %all-gather.11.cloned.1.call-done = bf16[1024,1024]{1,0:T(8,128)(2,1)} async-done(((bf16[32,1024]{1,0:T(8,128)(2,1)}), bf16[1024,1024]{1,0:T(8,128)(2,1)}) %all-gather.11.cloned.1.call-update) | async-done | bytes 2097168 | tf_op jit(solution)/shard_map/all_gather | solution.py:138
  215.4 3.2 fusion.50
  223.5 47.4 %all-gather.15.cloned.1.call-done = bf16[1024,1024]{1,0:T(8,128)(2,1)} async-done(((bf16[32,1024]{1,0:T(8,128)(2,1)}), bf16[1024,1024]{1,0:T(8,128)(2,1)}) %all-gather.15.cloned.1.call-update) | async-done | bytes 2097168 | tf_op jit(solution)/shard_map/all_gather | solution.py:151
  273.7 76.3 %all-gather.17.cloned.1.call-done = bf16[1024,4096]{1,0:T(8,128)(2,1)} async-done(((bf16[32,4096]{1,0:T(8,128)(2,1)}), bf16[1024,4096]{1,0:T(8,128)(2,1)}) %all-gather.17.cloned.1.call-update) | async-done | bytes 8388624 | tf_op jit(solution)/shard_map/all_gather | solution.py:159
  350.1 8.3 fusion.95
  358.4 70.5 %all-gather.19.cloned.1.call-done = bf16[4096,1024]{1,0:T(8,128)(2,1)} async-done(((bf16[128,1024]{1,0:T(8,128)(2,1)}), bf16[4096,1024]{1,0:T(8,128)(2,1)}) %all-gather.19.cloned.1.call-update) | async-done | bytes 8388624 | tf_op jit(solution)/shard_map/all_gather | solution.py:160
  428.9 7.5 fusion.109
  438.7 8.8 fusion.6
  447.5 2.8 multiply_reduce_fusion.2
  454.8 3.9 fusion.43
  462.2 2.7 fusion.91
  464.9 2.8 fusion.97
  467.7 3.7 multiply_reduce_fusion.3
  477.3 7.2 pad_maximum_fusion.1
  484.5 17.5 copy.129
  507.4 3.6 multiply_reduce_fusion
  517.3 7.2 pad_maximum_fusion
  524.4 17.6 copy.127
  542.1 11.1 fusion.89
  553.5 9.8 fusion.93
  566.8 3.5 fusion.37
  575.0 3.4 fusion.41
  578.3 26.8 %reduce-scatter.25.cloned.1.call-done = f32[32,3]{1,0:T(8,128)} async-done(((f32[1024,3]{1,0:T(8,128)}), f32[32,3]{1,0:T(8,128)}) %reduce-scatter.25.cloned.1.call-update) | async-done | bytes 400
  606.5 131.5 %reduce-scatter.23.cloned.1.call-done = f32[32,3]{1,0:T(8,128)} async-done(((f32[1024,3]{1,0:T(8,128)}), f32[32,3]{1,0:T(8,128)}) %reduce-scatter.23.cloned.1.call-update) | async-done | bytes 400
  739.3 355.4 %reduce-scatter.21.cloned.1.call-done = f32[32,4096]{1,0:T(8,128)} async-done(((f32[1024,4096]{1,0:T(8,128)}), f32[32,4096]{1,0:T(8,128)}) %reduce-scatter.21.cloned.1.call-update) | async-done | bytes 524304
  1097.5 356.7 %reduce-scatter.19.cloned.1.call-done = f32[32,4096]{1,0:T(8,128)} async-done(((f32[1024,4096]{1,0:T(8,128)}), f32[32,4096]{1,0:T(8,128)}) %reduce-scatter.19.cloned.1.call-update) | async-done | bytes 524304
  1460.0 354.4 %reduce-scatter.17.cloned.1.call-done = f32[128,1024]{1,0:T(8,128)} async-done(((f32[4096,1024]{1,0:T(8,128)}), f32[128,1024]{1,0:T(8,128)}) %reduce-scatter.17.cloned.1.call-update) | async-done | bytes 524304 | tf_op jit(solution)/shard_map/reduce_scatter | solution.py:176
  1814.4 360.1 %reduce-scatter.15.cloned.1.call-done = f32[32,4096]{1,0:T(8,128)} async-done(((f32[1024,4096]{1,0:T(8,128)}), f32[32,4096]{1,0:T(8,128)}) %reduce-scatter.15.cloned.1.call-update) | async-done | bytes 524304 | tf_op jit(solution)/shard_map/reduce_scatter | solution.py:179
  (190 shorter events, 77.4 us)
Async XLA Ops:
  7.2 141.0 %copy-start = (bf16[1,256,1024]{2,1,0:T(8,128)(2,1)S(1)}, bf16[1,256,1024]{2,1,0:T(8,128)(2,1)}, u32[]{:S(2)}) copy-start(bf16[1,256,1024]{2,1,0:T(8,128)(2,1)} %param.15) | copy-start | bytes 1572868
  7.2 140.9 %all-gather.13.cloned.1.call-start = ((), (), s32[]{:S(2)}) async-start(), calls=%async_computation.8 | async-start | bytes 6488064 | tf_op jit(solution)/shard_map/all_gather | solution.py:150
  7.9 146.3 %all-gather.9.cloned.1.call-start = ((), (), s32[]{:S(2)}) async-start(), calls=%async_computation.6 | async-start | bytes 6488064 | tf_op jit(solution)/shard_map/all_gather | solution.py:137
  8.7 204.0 %all-gather.11.cloned.1.call-start = ((), (), s32[]{:S(2)}) async-start(), calls=%async_computation.7 | async-start | bytes 2162688 | tf_op jit(solution)/shard_map/all_gather | solution.py:138
  9.4 261.5 %all-gather.15.cloned.1.call-start = ((), (), s32[]{:S(2)}) async-start(), calls=%async_computation.9 | async-start | bytes 2162688 | tf_op jit(solution)/shard_map/all_gather | solution.py:151
  10.0 340.1 %all-gather.17.cloned.1.call-start = ((), (), s32[]{:S(2)}) async-start(), calls=%async_computation.10 | async-start | bytes 8650752 | tf_op jit(solution)/shard_map/all_gather | solution.py:159
  10.6 418.3 %all-gather.19.cloned.1.call-start = ((), (), s32[]{:S(2)}) async-start(), calls=%async_computation.11 | async-start | bytes 8650752 | tf_op jit(solution)/shard_map/all_gather | solution.py:160
  11.2 593.9 %reduce-scatter.25.cloned.1.call-start = ((), (), s32[]{:S(2)}) async-start(), calls=%async_computation.17 | async-start | bytes 540672
  150.5 3.7 copy-start.23
  150.7 69.1 %copy-start.13 = (bf16[256,1024]{0,1:T(8,128)(2,1)}, bf16[256,1024]{0,1:T(8,128)(2,1)S(1)}, u32[]{:S(2)}) copy-start(bf16[256,1024]{0,1:T(8,128)(2,1)S(1)} %copy.105) | copy-start | bytes 1572868
  156.7 6.2 copy-start.9
  159.4 4.4 copy-start.11
  166.6 51.9 %copy-start.25 = (bf16[16,64,256]{2,1,0:T(8,128)(2,1)}, bf16[16,64,256]{2,1,0:T(8,128)(2,1)S(1)}, u32[]{:S(2)}) copy-start(bf16[16,64,256]{2,1,0:T(8,128)(2,1)S(1)} %fusion.60) | copy-start | bytes 1572868
  223.5 126.6 %copy-start.37 = (bf16[16,64,256]{2,1,0:T(8,128)(2,1)}, bf16[16,64,256]{2,1,0:T(8,128)(2,1)S(1)}, u32[]{:S(2)}) copy-start(bf16[16,64,256]{2,1,0:T(8,128)(2,1)S(1)} %fusion.59) | copy-start | bytes 1572868
  358.4 78.3 %copy-start.33 = (bf16[1,256,1024]{2,1,0:T(8,128)(2,1)S(1)}, bf16[1,256,1024]{2,1,0:T(8,128)(2,1)}, u32[]{:S(2)}) copy-start(bf16[1,256,1024]{2,1,0:T(8,128)(2,1)} %param.27) | copy-start | bytes 1572868
  437.3 10.1 slice-start
  438.7 8.8 copy-start.17
  438.7 8.8 slice-start.1
  447.5 4.2 copy-start.36
  454.8 3.9 copy-start.5
  454.8 3.9 copy-start.32
  472.4 265.5 %reduce-scatter.23.cloned.1.call-start = ((), (), s32[]{:S(2)}) async-start(), calls=%async_computation.16 | async-start | bytes 540672
  473.6 621.1 %reduce-scatter.21.cloned.1.call-start = ((), (), s32[]{:S(2)}) async-start(), calls=%async_computation.15 | async-start | bytes 17301504
  473.7 3.6 copy-start.7
  502.0 952.2 %reduce-scatter.19.cloned.1.call-start = ((), (), s32[]{:S(2)}) async-start(), calls=%async_computation.14 | async-start | bytes 17301504
  507.4 3.7 copy-start.3
  542.0 1272.4 %reduce-scatter.17.cloned.1.call-start = ((), (), s32[]{:S(2)}) async-start(), calls=%async_computation.13 | async-start | bytes 17301504 | tf_op jit(solution)/shard_map/reduce_scatter | solution.py:176
  553.2 1621.3 %reduce-scatter.15.cloned.1.call-start = ((), (), s32[]{:S(2)}) async-start(), calls=%async_computation.12 | async-start | bytes 17301504 | tf_op jit(solution)/shard_map/reduce_scatter | solution.py:179
  564.3 5.9 copy-start.29
  566.7 5.8 copy-start.20
  566.8 5.8 copy-start.35
  1094.7 1079.8 %copy-start.1 = (bf16[1,256,1024]{2,1,0:T(8,128)(2,1)S(1)}, bf16[1,256,1024]{2,1,0:T(8,128)(2,1)}, u32[]{:S(2)}) copy-start(bf16[1,256,1024]{2,1,0:T(8,128)(2,1)} %param.15) | copy-start | bytes 1572868
  (22 other events, 38.5 us)
Sparse Core Ops, SparseCore 0:
  11.1 71.9 all-gather.12
  86.1 68.0 all-gather.8
  157.2 55.4 all-gather.10
  215.5 55.3 all-gather.14
  273.8 76.2 all-gather.16
  352.9 75.9 all-gather.18
  472.6 132.4 reduce-scatter.24
  607.4 130.4 reduce-scatter.22
  740.2 354.4 reduce-scatter.20
  1096.8 357.3 reduce-scatter.18
  1457.1 357.3 reduce-scatter.16
  1817.2 357.2 reduce-scatter.14
where the time goes:
time: 2190 us; the launch traced here: 2180 us
  waiting for transfers between devices  1830 us (84%)
  blocking collectives  134 us (6%)
  matrix products  116 us (5%)
  local copies, waits for them, and re-layouts  61.5 us (3%)
  other arithmetic  24.6 us (1%)
    unnamed x16, waiting for transfers between devices  874 us
    reduce_scatter x1, waiting for transfers between devices, per_device(): lax.psum_scatter(product(second_low.T, grad_hidden), ('dp', 'fsdp'), scat...  360 us
    reduce_scatter x1, waiting for transfers between devices, per_device(): lax.psum_scatter(product(active.T, ffn_branch), ('dp', 'fsdp'), scatter_d...  354 us
    dot_general x27, matrix products, product(): return jnp.dot(first_side, other_side, preferred_element_type=jnp.float32)  101 us
    all_gather x1, waiting for transfers between devices, per_device(): lax.all_gather(widen_weight, ('dp', 'fsdp'), axis=0, tiled=True)  76.3 us
    all_gather x1, waiting for transfers between devices, per_device(): lax.all_gather(narrow_weight, ('dp', 'fsdp'), axis=0, tiled=True)  70.5 us
    all_gather x1, blocking collectives, per_device(): lax.all_gather(norm_gain, ('dp', 'fsdp'), axis=1, tiled=True)  70.4 us
    all_gather x1, blocking collectives, per_device(): lax.all_gather(norm_bias, ('dp', 'fsdp'), axis=1, tiled=True)  63.9 us
  transfers between devices with their start and end apart: 12, of which 10 were waited for; matrix products, arithmetic and copies ran while one was open for 7% of the time, Pallas kernels for 0%

commit v1 on v0

--- a/solution.py
+++ b/solution.py
@@ -1,6 +1,11 @@
+import functools
+
 import jax
 import jax.numpy as jnp
+import numpy as np
 from jax import lax
+from jax.experimental import pallas as pl
+from jax.experimental.pallas import tpu as pltpu
 from jax.sharding import PartitionSpec as P
 
 HEADS = 16
@@ -44,11 +49,6 @@
     grad_query_side = product(grad_query, weight_stack[0].T)
     grad_key_side = product(grad_key, weight_stack[1].T) + product(grad_value, weight_stack[2].T)
     return (grad_query_side, grad_key_side)
-
-
-def split_terms(terms, width):
-    stack_rows = terms[:, : 3 * width].reshape(terms.shape[0], 3, width).transpose(1, 0, 2)
-    return (stack_rows, terms[:, 3 * width :])
 
 
 def masked_scores(head_query, head_key, allowed):
@@ -102,7 +102,151 @@
     )
 
 
+AXES = ("dp", "fsdp")
+
+
+class Cube:
+    def __init__(self, mesh):
+        self.sizes = {axis: mesh.shape[axis] for axis in AXES}
+        self.count = self.sizes["dp"] * self.sizes["fsdp"]
+        inner = [("fsdp", k) for k in range(self.sizes["fsdp"].bit_length() - 1)]
+        outer = [("dp", k) for k in range(self.sizes["dp"].bit_length() - 1)]
+        self.place = {bit: k for k, bit in enumerate(inner + outer)}
+        core, outer = outer[0], outer[1:]
+        self.orders = {
+            "A": [core, inner[0], *outer, *inner[1:]],
+            "B": [core, *outer, *inner],
+            "C": [core, inner[1], inner[0], *outer, *inner[2:]],
+            "D": [core, inner[1], *outer, inner[0], *inner[2:]],
+        }
+
+    def index(self):
+        return lax.axis_index("dp") * self.sizes["fsdp"] + lax.axis_index("fsdp")
+
+    def swap(self, block, bit):
+        axis, k = bit
+        pairs = [(i, i ^ (1 << k)) for i in range(self.sizes[axis])]
+        return lax.ppermute(block, axis, pairs)
+
+    def offsets(self, name):
+        order = self.orders[name]
+        last = len(order) - 1
+        return [
+            sum(1 << self.place[bit] for k, bit in enumerate(order) if (p >> (last - k)) & 1)
+            for p in range(self.count)
+        ]
+
+    def gather(self, shard, name):
+        held = shard[None]
+        for bit in self.orders[name][:0:-1]:
+            held = jnp.concatenate([held, self.swap(held, bit)], axis=0)
+        return held, self.swap(held, self.orders[name][0])
+
+    def natural(self, halves, name):
+        low, high = halves
+        offsets = self.offsets(name)
+        count, half = self.count, self.count // 2
+        stack, rows, columns = low.shape[1:]
+        if rows % 16:
+            where = np.argsort(np.array(offsets))
+            picked = jnp.asarray(where)[jnp.arange(count) ^ self.index()]
+            blocks = jnp.take(jnp.concatenate(halves, axis=0), picked, axis=0)
+            return blocks.transpose(1, 0, 2, 3).reshape(stack, count * rows, columns)
+
+        def body(index_ref, low_ref, high_ref, out_ref, sems):
+            index = index_ref[0]
+            copies = []
+            for p in range(count):
+                source = low_ref.at[p] if p < half else high_ref.at[p - half]
+                copies.append(pltpu.make_async_copy(source, out_ref.at[:, index ^ offsets[p]], sems.at[p]))
+                copies[-1].start()
+            for copy in copies:
+                copy.wait()
+
+        moved = pl.pallas_call(
+            body,
+            out_shape=jax.ShapeDtypeStruct((stack, count, rows, columns), low.dtype),
+            in_specs=[
+                pl.BlockSpec(memory_space=pltpu.SMEM),
+                pl.BlockSpec(memory_space=pl.ANY),
+                pl.BlockSpec(memory_space=pl.ANY),
+            ],
+            out_specs=pl.BlockSpec(memory_space=pltpu.VMEM),
+            scratch_shapes=[pltpu.SemaphoreType.DMA((count,))],
+            compiler_params=pltpu.CompilerParams(vmem_limit_bytes=40 * 2**20),
+            name="natural_order",
+        )(self.index().astype(jnp.int32).reshape(1), low, high)
+        return moved.reshape(stack, count * rows, columns)
+
+    def turned(self, values_in, names):
+        tokens, features = values_in.shape
+        count, rows = self.count, features // self.count
+        tables = [self.offsets(name) for name in names]
+        if rows % 16:
+            blocks = values_in.T.reshape(count, rows, tokens)
+            return [jnp.take(blocks, jnp.asarray(table) ^ self.index(), axis=0) for table in tables]
+
+        def body(index_ref, in_ref, *refs):
+            index = index_ref[0]
+            outs, held = refs[:-1], refs[-1]
+            held[...] = in_ref[...].T.reshape(count, rows, tokens)
+            for table, out in zip(tables, outs):
+                for p in range(count):
+                    out[p] = held[index ^ table[p]]
+
+        shape = (count, rows, tokens)
+        return pl.pallas_call(
+            body,
+            out_shape=[jax.ShapeDtypeStruct(shape, values_in.dtype) for _ in tables],
+            in_specs=[pl.BlockSpec(memory_space=pltpu.SMEM), pl.BlockSpec(memory_space=pltpu.VMEM)],
+            out_specs=[pl.BlockSpec(memory_space=pltpu.VMEM) for _ in tables],
+            scratch_shapes=[pltpu.VMEM(shape, values_in.dtype)],
+            compiler_params=pltpu.CompilerParams(vmem_limit_bytes=40 * 2**20),
+            name="turned",
+        )(self.index().astype(jnp.int32).reshape(1), values_in)
+
+    def scatter(self, turned, other_side, name):
+        order = self.orders[name]
+        count, rows, tokens = turned.shape
+        half, quarter = count // 2, count // 4
+
+        def part(first, last):
+            return product(turned[first:last].reshape((last - first) * rows, tokens), other_side)
+
+        got = self.swap(rounded(part(half, count)), order[0])
+        sent = rounded(part(quarter, half) + got[quarter * rows :].astype(jnp.float32))
+        kept = part(0, quarter) + got[: quarter * rows].astype(jnp.float32)
+        for bit in order[1:-1]:
+            got = self.swap(sent, bit).astype(jnp.float32)
+            middle = kept.shape[0] // 2
+            sent = rounded(kept[middle:] + got[middle:])
+            kept = kept[:middle] + got[:middle]
+        return kept + self.swap(sent, order[-1]).astype(jnp.float32)
+
+    def scatter_small(self, rows_in):
+        lines, features = rows_in.shape
+        count = self.count
+        own = features // count
+        blocks = rows_in.reshape(lines, count, own).transpose(1, 0, 2)
+        blocks = jnp.pad(blocks, ((0, 0), (0, 8 - lines), (0, 128 - own)))
+        held = jnp.take(blocks, jnp.asarray(self.offsets("A")) ^ self.index(), axis=0)
+        for bit in self.orders["A"]:
+            middle = held.shape[0] // 2
+            held = held[:middle] + self.swap(held[middle:], bit)
+        return held[0, :lines, :own]
+
+    def gather_small(self, rows_in):
+        lines, own = rows_in.shape
+        block = jnp.pad(rows_in, ((0, 16 - lines), (0, 128 - own)))
+        held = jnp.concatenate(self.gather(block, "A"), axis=0)
+        where = np.argsort(np.array(self.offsets("A")))
+        picked = jnp.asarray(where)[jnp.arange(self.count) ^ self.index()]
+        held = jnp.take(held, picked, axis=0)[:, :lines, :own]
+        return held.transpose(1, 0, 2).reshape(lines, self.count * own)
+
+
 def per_device(
+    cube,
     tokens,
     memory,
     token_segments,
@@ -133,108 +277,125 @@
     cross_allowed = segment_row[:, None] == memory_segments[0][None, :]
     pad_scale = padding[0].astype(jnp.float32)[:, None]
     width = token_low.shape[1]
-    self_stack, self_final, gain_rows, bias_rows = (
-        lax.all_gather(self_project, ("dp", "fsdp"), axis=1, tiled=True),
-        lax.all_gather(self_output, ("dp", "fsdp"), axis=0, tiled=True),
-        lax.all_gather(norm_gain, ("dp", "fsdp"), axis=1, tiled=True),
-        lax.all_gather(norm_bias, ("dp", "fsdp"), axis=1, tiled=True),
-    )
-    gain_values = gain_rows.astype(jnp.float32)
-    bias_values = bias_rows.astype(jnp.float32)
+    own = self_project.shape[1]
+    spread = widen_weight.shape[1] // width
+    count = cube.count
+
+    packed = jnp.concatenate(
+        [
+            cross_project.reshape(3 * own, width),
+            cross_output,
+            widen_weight.reshape(own, spread, width).transpose(1, 0, 2).reshape(spread * own, width),
+            narrow_weight,
+        ],
+        axis=0,
+    )
+    later = lax.all_gather(packed, AXES, axis=0)
+    first_pair = cube.natural(cube.gather(self_project[:2], "A"), "A")
+    second_pair = cube.natural(
+        cube.gather(jnp.concatenate([self_project[2:], self_output[None]], axis=0), "B"), "B"
+    )
+    self_stack = [first_pair[0], first_pair[1], second_pair[0]]
+    self_final = second_pair[1]
+    norms = cube.gather_small(jnp.concatenate([norm_gain, norm_bias], axis=0)).astype(jnp.float32)
+    gain_values, bias_values = norms[:3], norms[3:]
+
     self_query, self_key, self_value = project_three(token_low, token_low, self_stack)
     self_mixed, self_logsum = attend_forward(self_query, self_key, self_value, self_allowed)
     pre_one = ALPHA * row_in + product(self_mixed, self_final)
     first_out = normalize(pre_one, gain_values[0], bias_values[0])
     first_low = rounded(first_out)
-    cross_stack, cross_final = (
-        lax.all_gather(cross_project, ("dp", "fsdp"), axis=1, tiled=True),
-        lax.all_gather(cross_output, ("dp", "fsdp"), axis=0, tiled=True),
-    )
+
+    cross_stack = [later[:, k * own : (k + 1) * own].reshape(width, width) for k in range(3)]
+    cross_final = later[:, 3 * own : 4 * own].reshape(width, width)
+    widen_full = (
+        later[:, 4 * own : (4 + spread) * own]
+        .reshape(count, spread, own, width)
+        .transpose(0, 2, 1, 3)
+        .reshape(width, spread * width)
+    )
+    narrow_full = later[:, (4 + spread) * own :].reshape(spread * width, width)
+
     cross_query, cross_key, cross_value = project_three(first_low, memory_low, cross_stack)
     cross_mixed, cross_logsum = attend_forward(cross_query, cross_key, cross_value, cross_allowed)
     pre_two = ALPHA * first_out + product(cross_mixed, cross_final)
     second = normalize(pre_two, gain_values[1], bias_values[1])
     second_low = rounded(second)
-    widen_full, narrow_full = (
-        lax.all_gather(widen_weight, ("dp", "fsdp"), axis=0, tiled=True),
-        lax.all_gather(narrow_weight, ("dp", "fsdp"), axis=0, tiled=True),
-    )
+
     hidden = product(second_low, widen_full)
     active = rounded(jax.nn.gelu(hidden))
     pre_three = ALPHA * second + product(active, narrow_full)
     third_out = normalize(pre_three, gain_values[2], bias_values[2])
     layer_out = rounded(third_out * pad_scale)
+
+    token_turned = cube.turned(token_low, ["A", "B"])
+    self_mixed_turned = cube.turned(self_mixed, ["D"])
+    first_turned = cube.turned(first_low, ["D"])
+    memory_turned = cube.turned(memory_low, ["B"])
+    cross_mixed_turned = cube.turned(cross_mixed, ["B"])
+    second_turned = cube.turned(second_low, ["C", "A"])
+    active_turned = cube.turned(active, ["A", "B"])
+
     grad_third = grad_out[0].astype(jnp.float32) * pad_scale
     grad_pre_three, grad_gain_three, grad_bias_three = normalize_back(
         pre_three, gain_values[2], bias_values[2], grad_third
     )
     ffn_branch = rounded(grad_pre_three)
+    middle = width // 2
+    narrow_parts = [
+        cube.scatter(active_turned[0], ffn_branch[:, :middle], "A"),
+        cube.scatter(active_turned[1], ffn_branch[:, middle:], "B"),
+    ]
     grad_active = product(ffn_branch, narrow_full.T)
     unused, gelu_pull = jax.vjp(jax.nn.gelu, hidden)
     grad_hidden = rounded(gelu_pull(grad_active)[0])
+    middle = grad_hidden.shape[1] // 2
+    widen_parts = [
+        cube.scatter(second_turned[0], grad_hidden[:, :middle], "C"),
+        cube.scatter(second_turned[1], grad_hidden[:, middle:], "A"),
+    ]
     grad_second = ALPHA * grad_pre_three + product(grad_hidden, widen_full.T)
-    grad_narrow = lax.psum_scatter(
-        product(active.T, ffn_branch), ("dp", "fsdp"), scatter_dimension=0, tiled=True
-    )
-    grad_widen = lax.psum_scatter(
-        product(second_low.T, grad_hidden), ("dp", "fsdp"), scatter_dimension=0, tiled=True
-    )
-    cross_stack, cross_final = (
-        lax.all_gather(cross_project, ("dp", "fsdp"), axis=1, tiled=True),
-        lax.all_gather(cross_output, ("dp", "fsdp"), axis=0, tiled=True),
-    )
-    cross_query, cross_key, cross_value = project_three(first_low, memory_low, cross_stack)
+
     grad_pre_two, grad_gain_two, grad_bias_two = normalize_back(
         pre_two, gain_values[1], bias_values[1], grad_second
     )
     cross_branch = rounded(grad_pre_two)
+    grad_cross_final = cube.scatter(cross_mixed_turned[0], cross_branch, "B")
     grad_mixed = rounded(product(cross_branch, cross_final.T))
     cross_dq, cross_dk, cross_dv = attend_backward(
         cross_query, cross_key, cross_value, cross_allowed, cross_logsum, grad_mixed
     )
     grad_first_in, grad_memory = project_inputs(cross_stack, cross_dq, cross_dk, cross_dv)
     grad_first = ALPHA * grad_pre_two + grad_first_in
-    cross_key_grads = jnp.concatenate([cross_dk, cross_dv], axis=1)
-    query_part = product(first_low.T, cross_dq)
-    memory_part = product(memory_low.T, cross_key_grads)
-    final_part = product(cross_mixed.T, cross_branch)
-    cross_rows = lax.psum_scatter(
-        jnp.concatenate([query_part, memory_part, final_part], axis=1),
-        ("dp", "fsdp"),
-        scatter_dimension=0,
-        tiled=True,
-    )
-    grad_cross_stack, grad_cross_final = split_terms(cross_rows, width)
-    self_stack, self_final = (
-        lax.all_gather(self_project, ("dp", "fsdp"), axis=1, tiled=True),
-        lax.all_gather(self_output, ("dp", "fsdp"), axis=0, tiled=True),
-    )
-    self_query, self_key, self_value = project_three(token_low, token_low, self_stack)
+    cross_key_rows = cube.scatter(memory_turned[0], jnp.concatenate([cross_dk, cross_dv], axis=1), "B")
+    cross_query_rows = cube.scatter(first_turned[0], cross_dq, "D")
+    grad_cross_stack = jnp.stack([cross_query_rows, cross_key_rows[:, :width], cross_key_rows[:, width:]])
+
     grad_pre_one, grad_gain_one, grad_bias_one = normalize_back(
         pre_one, gain_values[0], bias_values[0], grad_first
     )
     self_branch = rounded(grad_pre_one)
+    grad_self_final = cube.scatter(self_mixed_turned[0], self_branch, "D")
     grad_mixed = rounded(product(self_branch, self_final.T))
     self_dq, self_dk, self_dv = attend_backward(
         self_query, self_key, self_value, self_allowed, self_logsum, grad_mixed
     )
     grad_query_in, grad_key_in = project_inputs(self_stack, self_dq, self_dk, self_dv)
     grad_tokens = ALPHA * grad_pre_one + grad_query_in + grad_key_in
-    grad_gains = jnp.stack([grad_gain_one, grad_gain_two, grad_gain_three])
-    grad_biases = jnp.stack([grad_bias_one, grad_bias_two, grad_bias_three])
-    self_all_grads = jnp.concatenate([self_dq, self_dk, self_dv], axis=1)
-    input_part = product(token_low.T, self_all_grads)
-    final_part = product(self_mixed.T, self_branch)
-    self_rows = lax.psum_scatter(
-        jnp.concatenate([input_part, final_part], axis=1),
-        ("dp", "fsdp"),
-        scatter_dimension=0,
-        tiled=True,
-    )
-    grad_self_stack, grad_self_final = split_terms(self_rows, width)
-    grad_gains, grad_biases = (
-        lax.psum_scatter(grad_gains, ("dp", "fsdp"), scatter_dimension=1, tiled=True),
-        lax.psum_scatter(grad_biases, ("dp", "fsdp"), scatter_dimension=1, tiled=True),
+    self_value_rows = cube.scatter(token_turned[1], self_dv, "B")
+    self_key_rows = cube.scatter(token_turned[0], jnp.concatenate([self_dq, self_dk], axis=1), "A")
+    grad_self_stack = jnp.stack([self_key_rows[:, :width], self_key_rows[:, width:], self_value_rows])
+    grad_norms = cube.scatter_small(
+        jnp.stack(
+            [
+                grad_gain_one,
+                grad_gain_two,
+                grad_gain_three,
+                grad_bias_one,
+                grad_bias_two,
+                grad_bias_three,
+            ]
+        )
     )
     return (
         layer_out[None],
@@ -244,16 +405,16 @@
         grad_self_final,
         grad_cross_stack,
         grad_cross_final,
-        grad_widen,
-        grad_narrow,
-        grad_gains,
-        grad_biases,
+        jnp.concatenate(widen_parts, axis=1),
+        jnp.concatenate(narrow_parts, axis=1),
+        grad_norms[:3],
+        grad_norms[3:],
     )
 
 
 def solution(mesh):
     return jax.shard_map(
-        per_device,
+        functools.partial(per_device, Cube(mesh)),
         mesh=mesh,
         in_specs=(
             P(("dp", "fsdp"), None, None),

time: 2190 us -> 598 us (0.27)
  waiting for transfers between devices: 1830 us -> 283 us
  blocking collectives: 134 us -> 0 us
  starting transfers between devices: 0.94 us -> 57.6 us
  local copies, waits for them, and re-layouts: 61.5 us -> 92.3 us
    unnamed x16 -> x1, waiting for transfers between devices: 874 us -> 0.02 us
    reduce_scatter x2 -> x0, waiting for transfers between devices: 714 us -> none  [the longest x1 360 us: per_device(): lax.psum_scatter(product(second_low.T, grad_hidden), ('dp', 'fsdp'), scat...]
    ppermute x0 -> x70, waiting for transfers between devices: none -> 249 us  [swap(): return lax.ppermute(block, axis, pairs)]
    all_gather x6 -> x1, waiting for transfers between devices: 240 us -> 34.7 us  [per_device(): later = lax.all_gather(packed, AXES, axis=0)]
    all_gather x2 -> x0, blocking collectives: 134 us -> none  [the longest x1 70.4 us: per_device(): lax.all_gather(norm_gain, ('dp', 'fsdp'), axis=1, tiled=True)]
    ppermute x0 -> x70, starting transfers between devices: none -> 57.6 us  [swap(): return lax.ppermute(block, axis, pairs)]
    slice x4 -> x34, local copies, waits for them, and re-layouts: 5.24 us -> 32.4 us  [the longest x1 12.9 us: per_device(): narrow_full = later[:, (4 + spread) * own:].reshape(spread * width, width)]
    dot_general x27 -> x50, matrix products: 101 us -> 80 us  [product(): return jnp.dot(first_side, other_side, preferred_element_type=jnp.float32)]
  transfers between devices with their start and end apart: 12 -> 71, of which waited for: 10 -> 44; matrix products, arithmetic and copies ran while one was open for 7% -> 14% of each run, Pallas kernels for 0% -> 1%
where the time goes in v1:
time: 598 us; the launch traced here: 593 us
  waiting for transfers between devices  283 us (47%)
  matrix products  96.6 us (16%)
  local copies, waits for them, and re-layouts  92.3 us (15%)
  starting transfers between devices  57.6 us (10%)
  other arithmetic  37.9 us (6%)
  between operations  16.8 us (3%)
  Pallas kernels  8.33 us (1%)
    ppermute x70, waiting for transfers between devices, swap(): return lax.ppermute(block, axis, pairs)  249 us
    dot_general x50, matrix products, product(): return jnp.dot(first_side, other_side, preferred_element_type=jnp.float32)  80 us
    ppermute x70, starting transfers between devices, swap(): return lax.ppermute(block, axis, pairs)  57.6 us
    all_gather x1, waiting for transfers between devices, per_device(): later = lax.all_gather(packed, AXES, axis=0)  34.7 us
    unnamed x276, local copies, waits for them, and re-layouts  34.3 us
    slice x1, local copies, waits for them, and re-layouts, per_device(): narrow_full = later[:, (4 + spread) * own:].reshape(spread * width, width)  12.9 us
  transfers between devices with their start and end apart: 71, of which 44 were waited for; matrix products, arithmetic and copies ran while one was open for 14% of the time, Pallas kernels for 1%

profile of v1, /device:TPU:0, one launch (start us, length us, event | category | flops | bytes accessed | tf_op | source)
XLA Modules:
  0.0 592.9 jit_solution(6455471179993940078)
XLA Ops:
  10.4 4.1 collective-permute-start.10
  18.5 8.9 %collective-permute-done.5 = bf16[1,2,32,1024]{3,2,1,0:T(8,128)(2,1)S(1)} collective-permute-done((bf16[1,2,32,1024]{3,2,1,0:T(8,128)(2,1)S(1)}, bf16[1,2,32,1024]{3,2,1,0:T(8,128)(2,1)S(1)}, u32[]{:S(2)}, u32[]{:S(2)}) %collective-permute-start.5) | collective-permute-done | bytes 131104 | tf_op jit(solution)/shard_map/ppermute | solution.py:129
  27.5 5.6 collective-permute-done
  33.7 14.6 %collective-permute-done.6 = bf16[2,2,32,1024]{3,2,1,0:T(8,128)(2,1)S(1)} collective-permute-done((bf16[2,2,32,1024]{3,2,1,0:T(8,128)(2,1)S(1)}, bf16[2,2,32,1024]{3,2,1,0:T(8,128)(2,1)S(1)}, u32[]{:S(2)}, u32[]{:S(2)}) %collective-permute-start.6) | collective-permute-done | bytes 262176 | tf_op jit(solution)/shard_map/ppermute | solution.py:129
  50.6 6.4 %collective-permute-done.1 = bf16[2,2,32,1024]{3,2,1,0:T(8,128)(2,1)S(1)} collective-permute-done((bf16[2,2,32,1024]{3,2,1,0:T(8,128)(2,1)S(1)}, bf16[2,2,32,1024]{3,2,1,0:T(8,128)(2,1)S(1)}, u32[]{:S(2)}, u32[]{:S(2)}) %collective-permute-start.1) | collective-permute-done | bytes 262176 | tf_op jit(solution)/shard_map/ppermute | solution.py:129
  66.7 16.9 %collective-permute-done.2 = bf16[4,2,32,1024]{3,2,1,0:T(8,128)(2,1)} collective-permute-done((bf16[4,2,32,1024]{3,2,1,0:T(8,128)(2,1)}, bf16[4,2,32,1024]{3,2,1,0:T(8,128)(2,1)}, u32[]{:S(2)}, u32[]{:S(2)}) %collective-permute-start.2) | collective-permute-done | bytes 524320 | tf_op jit(solution)/shard_map/ppermute | solution.py:129
  91.4 14.0 %collective-permute-done.8 = bf16[8,2,32,1024]{3,2,1,0:T(8,128)(2,1)S(1)} collective-permute-done((bf16[8,2,32,1024]{3,2,1,0:T(8,128)(2,1)S(1)}, bf16[8,2,32,1024]{3,2,1,0:T(8,128)(2,1)S(1)}, u32[]{:S(2)}, u32[]{:S(2)}) %collective-permute-start.8) | collective-permute-done | bytes 1048608 | tf_op jit(solution)/shard_map/ppermute | solution.py:129
  112.9 4.6 collective-permute-done.11
  128.9 3.4 natural_order.3
  149.8 34.7 %all-gather.3.cloned.1.call-done = bf16[12288,1024]{1,0:T(8,128)(2,1)} async-done(((bf16[384,1024]{1,0:T(8,128)(2,1)}), bf16[12288,1024]{1,0:T(8,128)(2,1)}) %all-gather.3.cloned.1.call-update) | async-done | bytes 25165840 | tf_op jit(solution)/shard_map/all_gather | solution.py:293
  184.4 5.8 fusion.156
  190.2 12.9 %fusion.155 = (bf16[32,128,1024]{2,1,0:T(8,128)(2,1)}, bf16[32,128,1024]{2,1,0:T(8,128)(2,1)}) fusion(bf16[32,384,1024]{2,1,0:T(8,128)(2,1)} %bitcast.272), kind=kLoop, calls=%fused_computation.367 | loop fusion | bytes 33554432 | tf_op jit(solution)/shard_map/slice | solution.py:317
  218.0 11.4 %copy.72 = bf16[32,32,4,1024]{3,2,1,0:T(4,128)(2,1)} copy(bf16[32,32,4,1024]{3,1,2,0:T(8,128)(2,1)} %bitcast.270) | data formatting | bytes 16777216 | tf_op jit(solution)/shard_map/transpose | solution.py:314
  229.4 12.3 %copy.101 = bf16[128,8,4,1024]{3,1,2,0:T(8,128)(2,1)} copy(bf16[128,8,4,1024]{3,2,1,0:T(4,128)(2,1)} %bitcast.269) | data formatting | bytes 16777216
  241.7 8.7 %multiply_convert_fusion.2 = (bf16[256,4096]{1,0:T(8,128)(2,1)S(1)}, f32[256,4096]{1,0:T(8,128)}) fusion(bf16[256,1024]{1,0:T(8,128)(2,1)S(1)} %fusion.48.in_ref, bf16[1024,4096]{1,0:T(8,128)(2,1)} %bitcast.281), kind=kOutput, calls=%fused_computation.18 | convolution fusion | flops 2156920832 | bytes 15204352 | tf_op jit(solution)/shard_map/dot_general | solution.py:25
  253.4 6.0 %fusion.173 = (f32[256]{0:T(256)S(1)}, f32[256,1024]{1,0:T(8,128)S(1)}) fusion(bf16[256,4096]{1,0:T(8,128)(2,1)S(1)} %get-tuple-element.184.in_ref, bf16[4096,1024]{1,0:T(8,128)(2,1)} %bitcast.305, f32[1024]{0:T(1024)S(1)} %add.468, f32[1024]{0:T(1024)S(1)} %mul.322, f32[256]{0:T(256)S(1)} %fusion.137, f32[256,1024]{1,0:T(8,128)S(1)} %get-tuple-element.183, ...), kind=kOutput, calls=%fused_computation.385 | convolution fusion | flops 2149318400 | bytes 12594176 | tf_op jit(solution)/shard_map/dot_general | solution.py:25
  262.5 11.5 %fusion.6 = bf16[256,4096]{1,0:T(8,128)(2,1)S(1)} fusion(f32[256,4096]{1,0:T(8,128)} %get-tuple-element.185, bf16[256,1024]{1,0:T(8,128)(2,1)S(1)} %add_convert_fusion.12, bf16[4096,1024]{1,0:T(8,128)(2,1)} %bitcast.306), kind=kOutput, calls=%fused_computation.11 | convolution fusion | flops 2168455168 | bytes 15204352 | tf_op jit(solution)/shard_map/dot_general | solution.py:25
  351.1 3.3 collective-permute-done.68
  366.0 9.1 %collective-permute-done.41 = bf16[256,1024]{1,0:T(8,128)(2,1)S(1)} collective-permute-done((bf16[256,1024]{1,0:T(8,128)(2,1)S(1)}, bf16[256,1024]{1,0:T(8,128)(2,1)S(1)}, u32[]{:S(2)}, u32[]{:S(2)}) %collective-permute-start.41) | collective-permute-done | bytes 524320 | tf_op jit(solution)/shard_map/ppermute | solution.py:129
  378.8 9.2 %collective-permute-done.26 = bf16[256,1024]{1,0:T(8,128)(2,1)S(1)} collective-permute-done((bf16[256,1024]{1,0:T(8,128)(2,1)S(1)}, bf16[256,1024]{1,0:T(8,128)(2,1)S(1)}, u32[]{:S(2)}, u32[]{:S(2)}) %collective-permute-start.26) | collective-permute-done | bytes 524320 | tf_op jit(solution)/shard_map/ppermute | solution.py:129
  391.4 3.7 collective-permute-done.42
  420.7 6.2 %collective-permute-done.29 = bf16[32,1024]{1,0:T(8,128)(2,1)S(1)} collective-permute-done((bf16[32,1024]{1,0:T(8,128)(2,1)S(1)}, bf16[32,1024]{1,0:T(8,128)(2,1)S(1)}, u32[]{:S(2)}, u32[]{:S(2)}) %collective-permute-start.29) | collective-permute-done | bytes 65568 | tf_op jit(solution)/shard_map/ppermute | solution.py:129
  427.5 4.6 collective-permute-done.24
  449.4 13.8 %collective-permute-done.61 = bf16[1024,512]{0,1:T(8,128)(2,1)S(1)} collective-permute-done((bf16[1024,512]{0,1:T(8,128)(2,1)S(1)}, bf16[1024,512]{0,1:T(8,128)(2,1)S(1)}, u32[]{:S(2)}, u32[]{:S(2)}) %collective-permute-start.61) | collective-permute-done | bytes 1048608 | tf_op jit(solution)/shard_map/ppermute | solution.py:129
  467.1 20.9 %collective-permute-done.51 = bf16[256,2048]{1,0:T(8,128)(2,1)S(1)} collective-permute-done((bf16[256,2048]{1,0:T(8,128)(2,1)S(1)}, bf16[256,2048]{1,0:T(8,128)(2,1)S(1)}, u32[]{:S(2)}, u32[]{:S(2)}) %collective-permute-start.51) | collective-permute-done | bytes 1048608 | tf_op jit(solution)/shard_map/ppermute | solution.py:129
  492.4 18.1 %collective-permute-done.16 = bf16[256,2048]{1,0:T(8,128)(2,1)S(1)} collective-permute-done((bf16[256,2048]{1,0:T(8,128)(2,1)S(1)}, bf16[256,2048]{1,0:T(8,128)(2,1)S(1)}, u32[]{:S(2)}, u32[]{:S(2)}) %collective-permute-start.16) | collective-permute-done | bytes 1048608 | tf_op jit(solution)/shard_map/ppermute | solution.py:129
  511.6 10.1 %collective-permute-done.62 = bf16[512,512]{0,1:T(8,128)(2,1)S(1)} collective-permute-done((bf16[512,512]{0,1:T(8,128)(2,1)S(1)}, bf16[512,512]{0,1:T(8,128)(2,1)S(1)}, u32[]{:S(2)}, u32[]{:S(2)}) %collective-permute-start.62) | collective-permute-done | bytes 524320 | tf_op jit(solution)/shard_map/ppermute | solution.py:129
  524.9 8.0 %collective-permute-done.47 = bf16[128,2048]{1,0:T(8,128)(2,1)S(1)} collective-permute-done((bf16[128,2048]{1,0:T(8,128)(2,1)S(1)}, bf16[128,2048]{1,0:T(8,128)(2,1)S(1)}, u32[]{:S(2)}, u32[]{:S(2)}) %collective-permute-start.47) | collective-permute-done | bytes 524320 | tf_op jit(solution)/shard_map/ppermute | solution.py:129
  533.2 9.7 %collective-permute-done.37 = bf16[128,2048]{1,0:T(8,128)(2,1)S(1)} collective-permute-done((bf16[128,2048]{1,0:T(8,128)(2,1)S(1)}, bf16[128,2048]{1,0:T(8,128)(2,1)S(1)}, u32[]{:S(2)}, u32[]{:S(2)}) %collective-permute-start.37) | collective-permute-done | bytes 524320 | tf_op jit(solution)/shard_map/ppermute | solution.py:129
  550.1 11.2 %collective-permute-done.38 = bf16[64,2048]{1,0:T(8,128)(2,1)S(1)} collective-permute-done((bf16[64,2048]{1,0:T(8,128)(2,1)S(1)}, bf16[64,2048]{1,0:T(8,128)(2,1)S(1)}, u32[]{:S(2)}, u32[]{:S(2)}) %collective-permute-start.38) | collective-permute-done | bytes 262176 | tf_op jit(solution)/shard_map/ppermute | solution.py:129
  565.6 6.0 %collective-permute-done.54 = bf16[32,2048]{1,0:T(8,128)(2,1)S(1)} collective-permute-done((bf16[32,2048]{1,0:T(8,128)(2,1)S(1)}, bf16[32,2048]{1,0:T(8,128)(2,1)S(1)}, u32[]{:S(2)}, u32[]{:S(2)}) %collective-permute-start.54) | collective-permute-done | bytes 131104 | tf_op jit(solution)/shard_map/ppermute | solution.py:129
  574.7 4.1 collective-permute-done.39
  (658 shorter events, 256.5 us)
Async XLA Ops:
  7.3 177.2 %all-gather.3.cloned.1.call-start = ((), (), s32[]{:S(2)}) async-start(), calls=%async_computation | async-start | bytes 25952256 | tf_op jit(solution)/shard_map/all_gather | solution.py:293
  10.4 101.0 %collective-permute-start.10 = (bf16[1,16,128]{2,1,0:T(8,128)(2,1)S(1)}, bf16[1,16,128]{2,1,0:T(8,128)(2,1)S(1)}, u32[]{:S(2)}, u32[]{:S(2)}) collective-permute-start(bf16[1,16,128]{2,1,0:T(8,128)(2,1)S(1)} %fusion.135), channel_id=1, source_target_pairs={{0,4},{1,5},{2,6},{3,7},{4,0},{5,1},{6,2},{7,3},{8,12},{9,13},{10,... | collective-permute-start | bytes 12296 | tf_op jit(solution)/shard_map/ppermute | solution.py:129
  33.1 23.9 %collective-permute-start.1 = (bf16[2,2,32,1024]{3,2,1,0:T(8,128)(2,1)S(1)}, bf16[2,2,32,1024]{3,2,1,0:T(8,128)(2,1)S(1)}, u32[]{:S(2)}, u32[]{:S(2)}) collective-permute-start(bf16[2,2,32,1024]{3,2,1,0:T(8,128)(2,1)S(1)} %pad_maximum_fusion.25), channel_id=1, source_target_pairs={{0,2},{1,3},{2,0},{3,1},{4,6},{5,7},{6,4},{7,5},{8,10},{9,11},{10,... | collective-permute-start | bytes 786440 | tf_op jit(solution)/shard_map/ppermute | solution.py:129
  57.9 25.7 %collective-permute-start.2 = (bf16[4,2,32,1024]{3,2,1,0:T(8,128)(2,1)}, bf16[4,2,32,1024]{3,2,1,0:T(8,128)(2,1)}, u32[]{:S(2)}, u32[]{:S(2)}) collective-permute-start(bf16[4,2,32,1024]{3,2,1,0:T(8,128)(2,1)} %pad_maximum_fusion.5), channel_id=1, source_target_pairs={{0,1},{1,0},{2,3},{3,2},{4,5},{5,4},{6,7},{7,6},{8,9},{9,8},{10,11... | collective-permute-start | bytes 1572872 | tf_op jit(solution)/shard_map/ppermute | solution.py:129
  66.2 39.3 %collective-permute-start.8 = (bf16[8,2,32,1024]{3,2,1,0:T(8,128)(2,1)S(1)}, bf16[8,2,32,1024]{3,2,1,0:T(8,128)(2,1)S(1)}, u32[]{:S(2)}, u32[]{:S(2)}) collective-permute-start(bf16[8,2,32,1024]{3,2,1,0:T(8,128)(2,1)S(1)} %pad_maximum_fusion.1), channel_id=1, source_target_pairs={{0,1},{1,0},{2,3},{3,2},{4,5},{5,4},{6,7},{7,6},{8,9},{9,8},{10,11... | collective-permute-start | bytes 3145736 | tf_op jit(solution)/shard_map/ppermute | solution.py:129
  84.9 22.4 %collective-permute-start.3 = (bf16[8,2,32,1024]{3,2,1,0:T(8,128)(2,1)S(1)}, bf16[8,2,32,1024]{3,2,1,0:T(8,128)(2,1)S(1)}, u32[]{:S(2)}, u32[]{:S(2)}) collective-permute-start(bf16[8,2,32,1024]{3,2,1,0:T(8,128)(2,1)S(1)} %pad_maximum_fusion), channel_id=1, source_target_pairs={{0,16},{8,24},{16,0},{24,8},{1,17},{9,25},{17,1},{25,9},{2,18},{10... | collective-permute-start | bytes 3145736 | tf_op jit(solution)/shard_map/ppermute | solution.py:129
  105.6 23.4 %collective-permute-start.9 = (bf16[16,2,32,1024]{3,2,1,0:T(8,128)(2,1)S(1)}, bf16[16,2,32,1024]{3,2,1,0:T(8,128)(2,1)}, u32[]{:S(2)}, u32[]{:S(2)}) collective-permute-start(bf16[16,2,32,1024]{3,2,1,0:T(8,128)(2,1)S(1)} %constant_dynamic-update-slice_fusion.5.low_ref), channel_id=1, source_target_pairs={{0,8},{8,0},{16,24},{24,16},{1,9},{9,1},{17,25},{25,17},{2,10},{10... | collective-permute-start | bytes 6291464 | tf_op jit(solution)/shard_map/ppermute | solution.py:129
  108.3 24.0 %collective-permute-start.4 = (bf16[16,2,32,1024]{3,2,1,0:T(8,128)(2,1)}, bf16[16,2,32,1024]{3,2,1,0:T(8,128)(2,1)}, u32[]{:S(2)}, u32[]{:S(2)}) collective-permute-start(bf16[16,2,32,1024]{3,2,1,0:T(8,128)(2,1)} %constant_dynamic-update-slice_fusion.low_ref), channel_id=1, source_target_pairs={{0,8},{8,0},{16,24},{24,16},{1,9},{9,1},{17,25},{25,17},{2,10},{10... | collective-permute-start | bytes 6291464 | tf_op jit(solution)/shard_map/ppermute | solution.py:129
  316.1 42.9 %collective-permute-start.40 = (bf16[512,1024]{1,0:T(8,128)(2,1)}, bf16[512,1024]{1,0:T(8,128)(2,1)}, u32[]{:S(2)}, u32[]{:S(2)}) collective-permute-start(bf16[512,1024]{1,0:T(8,128)(2,1)} %convolution_convert_fusion.6), channel_id=1, source_target_pairs={{0,8},{8,0},{16,24},{24,16},{1,9},{9,1},{17,25},{25,17},{2,10},{10... | collective-permute-start | bytes 3145736 | tf_op jit(solution)/shard_map/ppermute | solution.py:129
  324.8 110.0 %collective-permute-start.60 = (bf16[2048,512]{0,1:T(8,128)(2,1)}, bf16[2048,512]{0,1:T(8,128)(2,1)}, u32[]{:S(2)}, u32[]{:S(2)}) collective-permute-start(bf16[2048,512]{0,1:T(8,128)(2,1)} %convolution_convert_fusion), channel_id=1, source_target_pairs={{0,8},{8,0},{16,24},{24,16},{1,9},{9,1},{17,25},{25,17},{2,10},{10... | collective-permute-start | bytes 6291464 | tf_op jit(solution)/shard_map/ppermute | solution.py:129
  334.0 27.2 %collective-permute-start.30 = (bf16[512,1024]{1,0:T(8,128)(2,1)S(1)}, bf16[512,1024]{1,0:T(8,128)(2,1)S(1)}, u32[]{:S(2)}, u32[]{:S(2)}) collective-permute-start(bf16[512,1024]{1,0:T(8,128)(2,1)S(1)} %convolution_convert_fusion.7), channel_id=1, source_target_pairs={{0,8},{8,0},{16,24},{24,16},{1,9},{9,1},{17,25},{25,17},{2,10},{10... | collective-permute-start | bytes 3145736 | tf_op jit(solution)/shard_map/ppermute | solution.py:129
  334.3 28.8 %collective-permute-start.25 = (bf16[512,1024]{1,0:T(8,128)(2,1)S(1)}, bf16[512,1024]{1,0:T(8,128)(2,1)S(1)}, u32[]{:S(2)}, u32[]{:S(2)}) collective-permute-start(bf16[512,1024]{1,0:T(8,128)(2,1)S(1)} %convolution_convert_fusion.8), channel_id=1, source_target_pairs={{0,8},{8,0},{16,24},{24,16},{1,9},{9,1},{17,25},{25,17},{2,10},{10... | collective-permute-start | bytes 3145736 | tf_op jit(solution)/shard_map/ppermute | solution.py:129
  359.0 78.1 %collective-permute-start.55 = (bf16[2048,512]{0,1:T(8,128)(2,1)S(1)}, bf16[2048,512]{0,1:T(8,128)(2,1)S(1)}, u32[]{:S(2)}, u32[]{:S(2)}) collective-permute-start(bf16[2048,512]{0,1:T(8,128)(2,1)S(1)} %copy-done.61), channel_id=1, source_target_pairs={{0,8},{8,0},{16,24},{24,16},{1,9},{9,1},{17,25},{25,17},{2,10},{10... | collective-permute-start | bytes 6291464 | tf_op jit(solution)/shard_map/ppermute | solution.py:129
  363.6 24.4 %collective-permute-start.26 = (bf16[256,1024]{1,0:T(8,128)(2,1)S(1)}, bf16[256,1024]{1,0:T(8,128)(2,1)S(1)}, u32[]{:S(2)}, u32[]{:S(2)}) collective-permute-start(bf16[256,1024]{1,0:T(8,128)(2,1)S(1)} %get-tuple-element.137), channel_id=1, source_target_pairs={{0,2},{1,3},{2,0},{3,1},{4,6},{5,7},{6,4},{7,5},{8,10},{9,11},{10,... | collective-permute-start | bytes 1572872 | tf_op jit(solution)/shard_map/ppermute | solution.py:129
  375.1 64.3 %collective-permute-start.50 = (bf16[512,2048]{1,0:T(8,128)(2,1)S(1)}, bf16[512,2048]{1,0:T(8,128)(2,1)S(1)}, u32[]{:S(2)}, u32[]{:S(2)}) collective-permute-start(bf16[512,2048]{1,0:T(8,128)(2,1)S(1)} %copy-done.60), channel_id=1, source_target_pairs={{0,8},{8,0},{16,24},{24,16},{1,9},{9,1},{17,25},{25,17},{2,10},{10... | collective-permute-start | bytes 6291464 | tf_op jit(solution)/shard_map/ppermute | solution.py:129
  417.4 23.2 %collective-permute-start.45 = (bf16[512,2048]{1,0:T(8,128)(2,1)S(1)}, bf16[512,2048]{1,0:T(8,128)(2,1)S(1)}, u32[]{:S(2)}, u32[]{:S(2)}) collective-permute-start(bf16[512,2048]{1,0:T(8,128)(2,1)S(1)} %copy-done.59), channel_id=1, source_target_pairs={{0,8},{8,0},{16,24},{24,16},{1,9},{9,1},{17,25},{25,17},{2,10},{10... | collective-permute-start | bytes 6291464 | tf_op jit(solution)/shard_map/ppermute | solution.py:129
  437.1 26.1 %collective-permute-start.61 = (bf16[1024,512]{0,1:T(8,128)(2,1)S(1)}, bf16[1024,512]{0,1:T(8,128)(2,1)S(1)}, u32[]{:S(2)}, u32[]{:S(2)}) collective-permute-start(bf16[1024,512]{0,1:T(8,128)(2,1)S(1)} %add_convert_fusion), channel_id=1, source_target_pairs={{0,16},{8,24},{16,0},{24,8},{1,17},{9,25},{17,1},{25,9},{2,18},{10... | collective-permute-start | bytes 3145736 | tf_op jit(solution)/shard_map/ppermute | solution.py:129
  439.4 26.1 %collective-permute-start.56 = (bf16[1024,512]{0,1:T(8,128)(2,1)S(1)}, bf16[1024,512]{0,1:T(8,128)(2,1)S(1)}, u32[]{:S(2)}, u32[]{:S(2)}) collective-permute-start(bf16[1024,512]{0,1:T(8,128)(2,1)S(1)} %add_convert_fusion.1), channel_id=1, source_target_pairs={{0,1},{1,0},{2,3},{3,2},{4,5},{5,4},{6,7},{7,6},{8,9},{9,8},{10,11... | collective-permute-start | bytes 3145736 | tf_op jit(solution)/shard_map/ppermute | solution.py:129
  440.6 47.4 %collective-permute-start.51 = (bf16[256,2048]{1,0:T(8,128)(2,1)S(1)}, bf16[256,2048]{1,0:T(8,128)(2,1)S(1)}, u32[]{:S(2)}, u32[]{:S(2)}) collective-permute-start(bf16[256,2048]{1,0:T(8,128)(2,1)S(1)} %add_convert_fusion.2), channel_id=1, source_target_pairs={{0,1},{1,0},{2,3},{3,2},{4,5},{5,4},{6,7},{7,6},{8,9},{9,8},{10,11... | collective-permute-start | bytes 3145736 | tf_op jit(solution)/shard_map/ppermute | solution.py:129
  442.5 46.3 %collective-permute-start.46 = (bf16[256,2048]{1,0:T(8,128)(2,1)S(1)}, bf16[256,2048]{1,0:T(8,128)(2,1)S(1)}, u32[]{:S(2)}, u32[]{:S(2)}) collective-permute-start(bf16[256,2048]{1,0:T(8,128)(2,1)S(1)} %add_convert_fusion.3), channel_id=1, source_target_pairs={{0,2},{1,3},{2,0},{3,1},{4,6},{5,7},{6,4},{7,5},{8,10},{9,11},{10,... | collective-permute-start | bytes 3145736 | tf_op jit(solution)/shard_map/ppermute | solution.py:129
  447.2 44.0 %collective-permute-start.36 = (bf16[256,2048]{1,0:T(8,128)(2,1)S(1)}, bf16[256,2048]{1,0:T(8,128)(2,1)S(1)}, u32[]{:S(2)}, u32[]{:S(2)}) collective-permute-start(bf16[256,2048]{1,0:T(8,128)(2,1)S(1)} %add_convert_fusion.4), channel_id=1, source_target_pairs={{0,16},{8,24},{16,0},{24,8},{1,17},{9,25},{17,1},{25,9},{2,18},{10... | collective-permute-start | bytes 3145736 | tf_op jit(solution)/shard_map/ppermute | solution.py:129
  463.1 47.3 %collective-permute-start.16 = (bf16[256,2048]{1,0:T(8,128)(2,1)S(1)}, bf16[256,2048]{1,0:T(8,128)(2,1)S(1)}, u32[]{:S(2)}, u32[]{:S(2)}) collective-permute-start(bf16[256,2048]{1,0:T(8,128)(2,1)S(1)} %add_convert_fusion.5), channel_id=1, source_target_pairs={{0,1},{1,0},{2,3},{3,2},{4,5},{5,4},{6,7},{7,6},{8,9},{9,8},{10,11... | collective-permute-start | bytes 3145736 | tf_op jit(solution)/shard_map/ppermute | solution.py:129
  465.5 56.2 %collective-permute-start.62 = (bf16[512,512]{0,1:T(8,128)(2,1)S(1)}, bf16[512,512]{0,1:T(8,128)(2,1)S(1)}, u32[]{:S(2)}, u32[]{:S(2)}) collective-permute-start(bf16[512,512]{0,1:T(8,128)(2,1)S(1)} %get-tuple-element.88), channel_id=1, source_target_pairs={{0,1},{1,0},{2,3},{3,2},{4,5},{5,4},{6,7},{7,6},{8,9},{9,8},{10,11... | collective-permute-start | bytes 1572872 | tf_op jit(solution)/shard_map/ppermute | solution.py:129
  488.0 34.2 %collective-permute-start.57 = (bf16[512,512]{0,1:T(8,128)(2,1)S(1)}, bf16[512,512]{0,1:T(8,128)(2,1)S(1)}, u32[]{:S(2)}, u32[]{:S(2)}) collective-permute-start(bf16[512,512]{0,1:T(8,128)(2,1)S(1)} %get-tuple-element.86), channel_id=1, source_target_pairs={{0,16},{8,24},{16,0},{24,8},{1,17},{9,25},{17,1},{25,9},{2,18},{10... | collective-permute-start | bytes 1572872 | tf_op jit(solution)/shard_map/ppermute | solution.py:129
  488.8 33.8 %collective-permute-start.52 = (bf16[128,2048]{1,0:T(8,128)(2,1)S(1)}, bf16[128,2048]{1,0:T(8,128)(2,1)S(1)}, u32[]{:S(2)}, u32[]{:S(2)}) collective-permute-start(bf16[128,2048]{1,0:T(8,128)(2,1)S(1)} %get-tuple-element.92), channel_id=1, source_target_pairs={{0,16},{8,24},{16,0},{24,8},{1,17},{9,25},{17,1},{25,9},{2,18},{10... | collective-permute-start | bytes 1572872 | tf_op jit(solution)/shard_map/ppermute | solution.py:129
  491.2 41.8 %collective-permute-start.47 = (bf16[128,2048]{1,0:T(8,128)(2,1)S(1)}, bf16[128,2048]{1,0:T(8,128)(2,1)S(1)}, u32[]{:S(2)}, u32[]{:S(2)}) collective-permute-start(bf16[128,2048]{1,0:T(8,128)(2,1)S(1)} %get-tuple-element.90), channel_id=1, source_target_pairs={{0,1},{1,0},{2,3},{3,2},{4,5},{5,4},{6,7},{7,6},{8,9},{9,8},{10,11... | collective-permute-start | bytes 1572872 | tf_op jit(solution)/shard_map/ppermute | solution.py:129
  510.5 32.4 %collective-permute-start.37 = (bf16[128,2048]{1,0:T(8,128)(2,1)S(1)}, bf16[128,2048]{1,0:T(8,128)(2,1)S(1)}, u32[]{:S(2)}, u32[]{:S(2)}) collective-permute-start(bf16[128,2048]{1,0:T(8,128)(2,1)S(1)} %get-tuple-element.94), channel_id=1, source_target_pairs={{0,1},{1,0},{2,3},{3,2},{4,5},{5,4},{6,7},{7,6},{8,9},{9,8},{10,11... | collective-permute-start | bytes 1572872 | tf_op jit(solution)/shard_map/ppermute | solution.py:129
  521.7 21.7 %collective-permute-start.17 = (bf16[128,2048]{1,0:T(8,128)(2,1)S(1)}, bf16[128,2048]{1,0:T(8,128)(2,1)S(1)}, u32[]{:S(2)}, u32[]{:S(2)}) collective-permute-start(bf16[128,2048]{1,0:T(8,128)(2,1)S(1)} %get-tuple-element.96), channel_id=1, source_target_pairs={{0,16},{8,24},{16,0},{24,8},{1,17},{9,25},{17,1},{25,9},{2,18},{10... | collective-permute-start | bytes 1572872 | tf_op jit(solution)/shard_map/ppermute | solution.py:129
  522.6 23.4 %collective-permute-start.58 = (bf16[256,512]{0,1:T(8,128)(2,1)S(1)}, bf16[256,512]{0,1:T(8,128)(2,1)S(1)}, u32[]{:S(2)}, u32[]{:S(2)}) collective-permute-start(bf16[256,512]{0,1:T(8,128)(2,1)S(1)} %get-tuple-element.102), channel_id=1, source_target_pairs={{0,2},{1,3},{2,0},{3,1},{4,6},{5,7},{6,4},{7,5},{8,10},{9,11},{10,... | collective-permute-start | bytes 786440 | tf_op jit(solution)/shard_map/ppermute | solution.py:129
  546.0 25.8 %collective-permute-start.64 = (bf16[128,512]{0,1:T(8,128)(2,1)S(1)}, bf16[128,512]{0,1:T(8,128)(2,1)S(1)}, u32[]{:S(2)}, u32[]{:S(2)}) collective-permute-start(bf16[128,512]{0,1:T(8,128)(2,1)S(1)} %fusion.82), channel_id=1, source_target_pairs={{0,4},{1,5},{2,6},{3,7},{4,0},{5,1},{6,2},{7,3},{8,12},{9,13},{10,... | collective-permute-start | bytes 393224 | tf_op jit(solution)/shard_map/ppermute | solution.py:129
  546.6 25.2 %collective-permute-start.59 = (bf16[128,512]{0,1:T(8,128)(2,1)S(1)}, bf16[128,512]{0,1:T(8,128)(2,1)S(1)}, u32[]{:S(2)}, u32[]{:S(2)}) collective-permute-start(bf16[128,512]{0,1:T(8,128)(2,1)S(1)} %fusion.84), channel_id=1, source_target_pairs={{0,4},{1,5},{2,6},{3,7},{4,0},{5,1},{6,2},{7,3},{8,12},{9,13},{10,... | collective-permute-start | bytes 393224 | tf_op jit(solution)/shard_map/ppermute | solution.py:129
  550.0 21.7 %collective-permute-start.54 = (bf16[32,2048]{1,0:T(8,128)(2,1)S(1)}, bf16[32,2048]{1,0:T(8,128)(2,1)S(1)}, u32[]{:S(2)}, u32[]{:S(2)}) collective-permute-start(bf16[32,2048]{1,0:T(8,128)(2,1)S(1)} %fusion.86), channel_id=1, source_target_pairs={{0,4},{1,5},{2,6},{3,7},{4,0},{5,1},{6,2},{7,3},{8,12},{9,13},{10,... | collective-permute-start | bytes 393224 | tf_op jit(solution)/shard_map/ppermute | solution.py:129
  (175 other events, 1576.2 us)
Sparse Core Ops, SparseCore 0:
  11.6 172.8 all-gather.2

commit v2 on v0

v2 whole, which is shorter than its diff:
```python
import functools

import jax
import jax.numpy as jnp
import numpy as np
from jax import lax
from jax.experimental import pallas as pl
from jax.experimental.pallas import tpu as pltpu
from jax.sharding import PartitionSpec as P

HEADS = 16
HEAD = 64


ALPHA = (3.0 * 200.0) ** 0.25
EPSILON = 1e-05
MASKED = -1e30


def rounded(values_in):
    return values_in.astype(jnp.bfloat16)


def product(first_side, other_side):
    return jnp.dot(first_side, other_side, preferred_element_type=jnp.float32)


AXES = ("far", "pair", "core", "fsdp")
PAIR = ("pair", 0)
CORE = ("core", 0)
GATHER_DEPTH = 2
SCATTER_DEPTH = 2
GATHER = {"s1": "A", "s2": "B", "c1": "A", "c2": "B"}
SCATTER = {"N": "E", "W": "F", "P1": "B", "P2": "D", "S1": "A", "S2": "B"}
STEPS = {
    "start": [],
    "early": ["s1", "s2", "s1", "s2"],
    "self": ["c1", "c2", "s1", "s2", "c1", "c2", "widen", "s1", "s2", "c1", "c2", "s1", "s2"],
    "cross": ["c1", "c2", "narrow", "c1", "c2"],
    "gs": ["W", "N"],
    "gf": ["P2", "P1", "W", "N"],
    "tail": ["P2", "P1", "S1", "S2", "W", "N", "P2", "S1", "S2", "W", "N", "P1", "P2", "S1", "S2", "W", "P1", "P2", "S1", "S2", "P1", "S1", "S2"],
}


def normalize(values_in, scale_row, shift_row):
    average = jnp.mean(values_in, axis=-1, keepdims=True)
    centred = values_in - average
    spread = jnp.mean(centred * centred, axis=-1, keepdims=True)
    return centred * lax.rsqrt(spread + EPSILON) * scale_row + shift_row


def normalize_back(values_in, scale_row, shift_row, grad_result):
    unused, pullback = jax.vjp(normalize, values_in, scale_row, shift_row)
    return pullback(grad_result)


def project_three(query_source, key_source, weight_stack):
    return (
        rounded(product(query_source, weight_stack[0])),
        rounded(product(key_source, weight_stack[1])),
        rounded(product(key_source, weight_stack[2])),
    )


def project_inputs(weight_stack, grad_query, grad_key, grad_value):
    grad_query_side = product(grad_query, weight_stack[0].T)
    grad_key_side = product(grad_key, weight_stack[1].T) + product(grad_value, weight_stack[2].T)
    return (grad_query_side, grad_key_side)


def masked_scores(head_query, head_key, allowed):
    scores = jnp.einsum(
        "qhd,khd->hqk", head_query, head_key, preferred_element_type=jnp.float32
    ) * HEAD ** (-0.5)
    return jnp.where(allowed[None], scores, MASKED)


def attend_forward(queries, key_rows, values, allowed):
    length = queries.shape[0]
    key_count = key_rows.shape[0]
    head_query = queries.reshape(length, HEADS, HEAD)
    head_key = key_rows.reshape(key_count, HEADS, HEAD)
    head_value = values.reshape(key_count, HEADS, HEAD)
    scores = masked_scores(head_query, head_key, allowed)
    largest = jnp.max(scores, axis=-1, keepdims=True)
    exponentials = jnp.exp(scores - largest)
    totals = jnp.sum(exponentials, axis=-1, keepdims=True)
    weights = rounded(exponentials / totals)
    mixed = jnp.einsum("hqk,khd->qhd", weights, head_value, preferred_element_type=jnp.float32)
    return (rounded(mixed.reshape(length, HEADS * HEAD)), largest + jnp.log(totals))


def attend_backward(queries, key_rows, values, allowed, logsum, grad_mixed):
    length = queries.shape[0]
    key_count = key_rows.shape[0]
    head_query = queries.reshape(length, HEADS, HEAD)
    head_key = key_rows.reshape(key_count, HEADS, HEAD)
    head_value = values.reshape(key_count, HEADS, HEAD)
    head_grad = grad_mixed.reshape(length, HEADS, HEAD)
    weights = jnp.exp(masked_scores(head_query, head_key, allowed) - logsum)
    grad_values = jnp.einsum(
        "hqk,qhd->khd", rounded(weights), head_grad, preferred_element_type=jnp.float32
    )
    grad_weights = jnp.einsum(
        "qhd,khd->hqk", head_grad, head_value, preferred_element_type=jnp.float32
    )
    inner_sum = jnp.sum(weights * grad_weights, axis=-1, keepdims=True)
    grad_scores = rounded(weights * (grad_weights - inner_sum))
    grad_queries = jnp.einsum(
        "hqk,khd->qhd", grad_scores, head_key, preferred_element_type=jnp.float32
    ) * HEAD ** (-0.5)
    grad_keys = jnp.einsum(
        "hqk,qhd->khd", grad_scores, head_query, preferred_element_type=jnp.float32
    ) * HEAD ** (-0.5)
    return (
        rounded(grad_queries.reshape(length, HEADS * HEAD)),
        rounded(grad_keys.reshape(key_count, HEADS * HEAD)),
        rounded(grad_values.reshape(key_count, HEADS * HEAD)),
    )


class Cube:
    def __init__(self, mesh):
        far, inner = mesh.shape["dp"] // 4, mesh.shape["fsdp"]
        self.mesh = jax.sharding.Mesh(mesh.devices.reshape(far, 2, 2, inner), AXES)
        self.sizes = dict(zip(AXES, (far, 2, 2, inner)))
        self.count = 4 * far * inner
        self.far = far
        close = [("fsdp", k) for k in range(inner.bit_length() - 1)]
        apart = [("far", k) for k in range(far.bit_length() - 1)]
        self.place = {bit: k for k, bit in enumerate([*close, CORE, PAIR, *apart])}
        self.side_place = {bit: k for k, bit in enumerate([*close, CORE, *apart])}
        self.orders = {
            "A": [CORE, close[0], PAIR, *close[1:], *apart],
            "B": [CORE, PAIR, *close, *apart],
            "C": [CORE, close[1], close[0], PAIR, *close[2:], *apart],
            "D": [CORE, close[1], PAIR, close[0], *close[2:], *apart],
            "E": [CORE, *close, *apart],
            "F": [CORE, close[1], close[0], *close[2:], *apart],
        }

    def index(self, place):
        return sum(((lax.axis_index(axis) >> k) & 1) << shift for (axis, k), shift in place.items())

    def swap(self, block, bit):
        axis, k = bit
        return lax.ppermute(block, axis, [(i, i ^ (1 << k)) for i in range(self.sizes[axis])])

    def offsets(self, order, place):
        last = len(order) - 1
        return [
            sum(1 << place[bit] for k, bit in enumerate(order) if (p >> (last - k)) & 1)
            for p in range(1 << len(order))
        ]

    def gather(self, shard, order):
        held = shard[None]
        for bit in order[:0:-1]:
            held = jnp.concatenate([held, (yield held, bit)], axis=0)
        return held, (yield held, order[0])

    def natural(self, halves, order, segments):
        low, high = halves
        offsets = self.offsets(order, self.place)
        count, half = self.count, self.count // 2
        columns = low.shape[2]
        starts = [sum(segments[:k]) for k in range(len(segments))]
        if any(rows % 16 for rows in segments):
            where = np.argsort(np.array(offsets))
            picked = jnp.asarray(where)[jnp.arange(count) ^ self.index(self.place)]
            blocks = jnp.take(jnp.concatenate(halves, axis=0), picked, axis=0)
            return [
                blocks[:, start : start + rows].reshape(count * rows, columns)
                for start, rows in zip(starts, segments)
            ]
        pieces = list(enumerate(zip(starts, segments)))

        def body(index_ref, low_ref, high_ref, *refs):
            index, sems = index_ref[0], refs[-1]
            copies = []
            for p in range(count):
                source = low_ref.at[p] if p < half else high_ref.at[p - half]
                for k, (start, rows) in pieces:
                    copies.append(
                        pltpu.make_async_copy(
                            source.at[pl.ds(start, rows)], refs[k].at[index ^ offsets[p]], sems.at[p, k]
                        )
                    )
                    copies[-1].start()
            for copy in copies:
                copy.wait()

        moved = pl.pallas_call(
            body,
            out_shape=[jax.ShapeDtypeStruct((count, rows, columns), low.dtype) for rows in segments],
            in_specs=[
                pl.BlockSpec(memory_space=pltpu.SMEM),
                pl.BlockSpec(memory_space=pl.ANY),
                pl.BlockSpec(memory_space=pl.ANY),
            ],
            out_specs=[pl.BlockSpec(memory_space=pltpu.VMEM) for _ in segments],
            scratch_shapes=[pltpu.SemaphoreType.DMA((count, len(segments)))],
            compiler_params=pltpu.CompilerParams(vmem_limit_bytes=40 * 2**20),
            name="natural_order",
        )(self.index(self.place).astype(jnp.int32).reshape(1), low, high)
        return [block.reshape(count * rows, columns) for block, rows in zip(moved, segments)]

    def turned(self, sources, orders, place):
        tokens, features = sources[0].shape
        count = 1 << len(place)
        rows, wide = features // count, tokens * len(sources)
        tables = [self.offsets(order, place) for order in orders]
        index = self.index(place)
        if rows % 16:
            blocks = jnp.concatenate(sources, axis=0).T.reshape(count, rows, wide)
            return [jnp.take(blocks, jnp.asarray(table) ^ index, axis=0) for table in tables]

        def body(index_ref, *refs):
            index = index_ref[0]
            ins, outs, held = refs[: len(sources)], refs[len(sources) : -1], refs[-1]
            for k, in_ref in enumerate(ins):
                held[:, :, pl.ds(k * tokens, tokens)] = in_ref[...].T.reshape(count, rows, tokens)
            for table, out in zip(tables, outs):
                for p in range(count):
                    out[p] = held[index ^ table[p]]

        shape = (count, rows, wide)
        return pl.pallas_call(
            body,
            out_shape=[jax.ShapeDtypeStruct(shape, sources[0].dtype) for _ in tables],
            in_specs=[pl.BlockSpec(memory_space=pltpu.SMEM)]
            + [pl.BlockSpec(memory_space=pltpu.VMEM) for _ in sources],
            out_specs=[pl.BlockSpec(memory_space=pltpu.VMEM) for _ in tables],
            scratch_shapes=[pltpu.VMEM(shape, sources[0].dtype)],
            compiler_params=pltpu.CompilerParams(vmem_limit_bytes=40 * 2**20),
            name="turned",
        )(index.astype(jnp.int32).reshape(1), *sources)

    def scatter(self, sides, order, extra=None):
        blocks = 1 << len(order)
        half, quarter = blocks // 2, blocks // 4

        def parts(first, last, got=None):
            terms, column = [], 0
            for turned, other in sides:
                rows = turned.shape[0] // blocks
                block = turned[first * rows : last * rows]
                term = product(block.reshape(-1, turned.shape[-1]), other)
                if got is not None:
                    term = term + got[:, column : column + term.shape[1]].astype(jnp.float32)
                column += term.shape[1]
                terms.append(term)
            if extra is not None:
                rows = extra.shape[0] // blocks
                term = extra[first * rows : last * rows]
                if got is not None:
                    term = term + got[:, column:].astype(jnp.float32)
                terms.append(term)
            return terms

        def joined(terms):
            return terms[0] if len(terms) == 1 else jnp.concatenate(terms, axis=1)

        got = yield joined([rounded(term) for term in parts(half, blocks)]), order[0]
        middle = got.shape[0] // 2
        sent = joined([rounded(term) for term in parts(quarter, half, got[middle:])])
        kept = joined(parts(0, quarter, got[:middle]))
        for bit in order[1:-1]:
            got = yield sent, bit
            middle = kept.shape[0] // 2
            sent = rounded(kept[middle:] + got[middle:].astype(jnp.float32))
            kept = kept[:middle] + got[:middle].astype(jnp.float32)
        return kept + (yield sent, order[-1]).astype(jnp.float32)

    def scatter_pair(self, sides, order):
        kept = yield from self.scatter(sides, order)
        middle = kept.shape[0] // 2
        got = (yield rounded(kept[middle:]), PAIR).astype(jnp.float32)
        return kept[:middle], got


    def columns(self, vectors, order):
        lines, features = vectors.shape
        own = features // self.count
        blocks = jnp.pad(vectors.T, ((0, 0), (0, 128 - lines))).reshape(self.count, own, 128)
        table = jnp.asarray(self.offsets(order, self.place))
        return jnp.take(blocks, table ^ self.index(self.place), axis=0).reshape(features, 128)


class Driver:
    def __init__(self, cube, depth):
        self.cube, self.depth = cube, depth
        self.before = {bit: [] for bit in cube.place}
        self.chains, self.got, self.results = {}, {}, {}
        self.token = None
        self.hooks = {}

    def swap(self, block, bit):
        past = self.before[bit]
        if len(past) >= self.depth:
            block, _ = lax.optimization_barrier((block, past[-self.depth]))
        past.append(self.cube.swap(block, bit))
        return past[-1]

    def after(self, block):
        if self.token is None:
            return block
        return lax.optimization_barrier((block, self.token))[0]

    def done(self, block):
        self.token = block
        return block

    def add(self, name, chain):
        self.chains[name] = chain
        block, bit = next(chain)
        self.token = block
        self.got[name] = self.swap(block, bit)

    def advance(self, names):
        for name in names:
            if name in self.hooks:
                self.results[name] = self.hooks.pop(name)()
            if name in self.results:
                continue
            got = self.after(self.got[name])
            try:
                block, bit = self.chains[name].send(got)
            except StopIteration as stop:
                self.results[name] = stop.value
                continue
            self.token = block
            self.got[name] = self.swap(block, bit)

    def finish(self, names):
        while left := [name for name in names if name not in self.results]:
            self.advance(left)
        return [self.results[name] for name in names]


def per_device(
    cube,
    tokens,
    memory,
    token_segments,
    memory_segments,
    padding,
    self_project,
    self_output,
    cross_project,
    cross_output,
    widen_weight,
    narrow_weight,
    norm_gain,
    norm_bias,
    grad_out,
):
    token_low = tokens[0]
    memory_low = memory[0]
    row_in = token_low.astype(jnp.float32)
    segment_row = token_segments[0]
    places = jnp.arange(segment_row.shape[0])
    diagonal = places[None, :] == places[:, None]
    live_keys = padding[0] == 1
    self_allowed = (
        (segment_row[:, None] == segment_row[None, :])
        & (places[None, :] <= places[:, None])
        & (live_keys[None, :] | diagonal)
    )
    cross_allowed = segment_row[:, None] == memory_segments[0][None, :]
    pad_scale = padding[0].astype(jnp.float32)[:, None]
    width = token_low.shape[1]
    own = self_project.shape[1]
    hidden_width = widen_weight.shape[1]
    count, far = cube.count, cube.far
    orders = cube.orders
    side = lax.axis_index("pair")
    drive = Driver(cube, GATHER_DEPTH)

    def both_sides(mine, other):
        return [jnp.where(side == 0, mine, other), jnp.where(side == 0, other, mine)]

    shard = widen_weight.reshape(own, far, 2, hidden_width // (2 * far))
    mine, other = (
        lax.dynamic_index_in_dim(shard, k, axis=2, keepdims=False).reshape(own, hidden_width // 2)
        for k in (side, 1 - side)
    )
    widen_shard = jnp.stack(both_sides(mine, drive.swap(other, PAIR)))

    def gather_widen():
        full = lax.all_gather(drive.after(widen_shard), ("far", "core", "fsdp"), axis=1, tiled=True)
        return (
            full.reshape(2, far, width // (2 * far), hidden_width // 2)
            .transpose(1, 0, 2, 3)
            .reshape(width, hidden_width // 2)
        )

    def gather_narrow():
        return lax.all_gather(drive.after(narrow_weight), ("far", "core", "fsdp"), axis=0, tiled=True)

    drive.hooks = {"widen": gather_widen, "narrow": gather_narrow}
    drive.advance(STEPS["start"])
    norm_rows = jnp.concatenate([norm_gain, norm_bias], axis=0)
    norm_rows = jnp.pad(norm_rows, ((0, 16 - 6), (0, width - own)))
    drive.add("s1", cube.gather(self_project[:2].reshape(2 * own, width), orders[GATHER["s1"]]))
    drive.add(
        "s2",
        cube.gather(
            jnp.concatenate([self_project[2], self_output, norm_rows], axis=0), orders[GATHER["s2"]]
        ),
    )
    drive.advance(STEPS["early"])
    drive.add("c1", cube.gather(cross_project[:2].reshape(2 * own, width), orders[GATHER["c1"]]))
    drive.add(
        "c2",
        cube.gather(jnp.concatenate([cross_project[2], cross_output], axis=0), orders[GATHER["c2"]]),
    )
    drive.advance(STEPS["self"])
    drive.finish(["s1", "s2"])
    query_full, key_full = cube.natural(drive.results["s1"], orders[GATHER["s1"]], [own, own])
    value_full, self_final, norms = cube.natural(drive.results["s2"], orders[GATHER["s2"]], [own, own, 16])
    self_stack = [query_full, key_full, value_full]
    norms = norms.reshape(count, 16, width)[:, :6, :own].transpose(1, 0, 2).reshape(6, width)
    norms = norms.astype(jnp.float32)
    gain_values, bias_values = norms[:3], norms[3:]

    self_query, self_key, self_value = project_three(token_low, token_low, self_stack)
    self_mixed, self_logsum = attend_forward(self_query, self_key, self_value, self_allowed)
    pre_one = ALPHA * row_in + product(self_mixed, self_final)
    first_out = normalize(pre_one, gain_values[0], bias_values[0])
    first_low = rounded(first_out)

    drive.done(first_low)
    drive.advance(STEPS["cross"])
    drive.finish(["c1", "c2"])
    widen_full, narrow_full = drive.finish(["widen", "narrow"])
    query_full, key_full = cube.natural(drive.results["c1"], orders[GATHER["c1"]], [own, own])
    value_full, cross_final = cube.natural(drive.results["c2"], orders[GATHER["c2"]], [own, own])
    cross_stack = [query_full, key_full, value_full]
    cross_query, cross_key, cross_value = project_three(first_low, memory_low, cross_stack)
    cross_mixed, cross_logsum = attend_forward(cross_query, cross_key, cross_value, cross_allowed)
    pre_two = ALPHA * first_out + product(cross_mixed, cross_final)
    second = normalize(pre_two, gain_values[1], bias_values[1])
    second_low = rounded(second)

    def widened(rows_low):
        hidden = product(rows_low, widen_full)
        active = rounded(jax.nn.gelu(hidden))
        return hidden, active, product(active, narrow_full)

    second_other = cube.swap(second_low, PAIR)
    hidden, active, branch = widened(second_low)
    hidden_other, active_other, branch_other = widened(second_other)
    branch_got = cube.swap(rounded(branch_other), PAIR)
    pre_three = ALPHA * second + (branch + branch_got.astype(jnp.float32))
    third_out = normalize(pre_three, gain_values[2], bias_values[2])
    layer_out = rounded(third_out * pad_scale)

    (self_mixed_turned,) = cube.turned([self_mixed], [orders[SCATTER["S2"]]], cube.place)
    token_turned = cube.turned([token_low], [orders[SCATTER["S1"]], orders[SCATTER["S2"]]], cube.place)
    (first_turned,) = cube.turned([first_low], [orders[SCATTER["P2"]]], cube.place)
    (memory_turned,) = cube.turned([memory_low], [orders[SCATTER["P1"]]], cube.place)
    (cross_mixed_turned,) = cube.turned([cross_mixed], [orders[SCATTER["P2"]]], cube.place)
    (second_turned,) = cube.turned([second_low, second_other], [[*orders[SCATTER["W"]], PAIR]], cube.place)
    (active_turned,) = cube.turned([active, active_other], [orders[SCATTER["N"]]], cube.side_place)
    drive = Driver(cube, SCATTER_DEPTH)

    grad_third = grad_out[0].astype(jnp.float32) * pad_scale
    grad_pre_three, grad_gain_three, grad_bias_three = normalize_back(
        pre_three, gain_values[2], bias_values[2], grad_third
    )
    ffn_branch = rounded(grad_pre_three)

    def widened_back(branch_low, hidden):
        grad_active = product(branch_low, narrow_full.T)
        unused, gelu_pull = jax.vjp(jax.nn.gelu, hidden)
        grad_hidden = rounded(gelu_pull(grad_active)[0])
        return grad_hidden, product(grad_hidden, widen_full.T)

    ffn_branch_other = cube.swap(ffn_branch, PAIR)
    grad_hidden, grad_branch = widened_back(ffn_branch, hidden)
    grad_hidden_other, grad_branch_other = widened_back(ffn_branch_other, hidden_other)
    grad_branch_got = drive.swap(drive.done(rounded(grad_branch_other)), PAIR)
    drive.add(
        "N",
        cube.scatter(
            [(drive.after(active_turned), jnp.concatenate([ffn_branch, ffn_branch_other], axis=0))], orders[SCATTER["N"]]
        ),
    )
    drive.add(
        "W",
        cube.scatter_pair(
            [(drive.after(second_turned), jnp.concatenate([grad_hidden, grad_hidden_other], axis=0))],
            orders[SCATTER["W"]],
        ),
    )
    grad_branch_got = drive.after(grad_branch_got)
    grad_second = ALPHA * grad_pre_three + (grad_branch + grad_branch_got.astype(jnp.float32))

    grad_pre_two, grad_gain_two, grad_bias_two = normalize_back(
        pre_two, gain_values[1], bias_values[1], grad_second
    )
    cross_branch = drive.done(rounded(grad_pre_two))
    drive.advance(STEPS["gs"])
    cross_branch = drive.after(cross_branch)
    grad_mixed = rounded(product(cross_branch, cross_final.T))
    cross_dq, cross_dk, cross_dv = attend_backward(
        cross_query, cross_key, cross_value, cross_allowed, cross_logsum, grad_mixed
    )
    grad_first_in, grad_memory = project_inputs(cross_stack, cross_dq, cross_dk, cross_dv)
    grad_first = ALPHA * grad_pre_two + grad_first_in
    drive.add(
        "P1",
        cube.scatter([(memory_turned, jnp.concatenate([cross_dk, cross_dv], axis=1))], orders[SCATTER["P1"]]),
    )
    drive.add(
        "P2",
        cube.scatter([(first_turned, cross_dq), (cross_mixed_turned, cross_branch)], orders[SCATTER["P2"]]),
    )
    drive.advance(STEPS["gf"])
    grad_first = drive.after(grad_first)

    grad_pre_one, grad_gain_one, grad_bias_one = normalize_back(
        pre_one, gain_values[0], bias_values[0], grad_first
    )
    self_branch = rounded(grad_pre_one)
    grad_mixed = rounded(product(self_branch, self_final.T))
    self_dq, self_dk, self_dv = attend_backward(
        self_query, self_key, self_value, self_allowed, self_logsum, grad_mixed
    )
    grad_query_in, grad_key_in = project_inputs(self_stack, self_dq, self_dk, self_dv)
    grad_tokens = ALPHA * grad_pre_one + grad_query_in + grad_key_in
    grad_norms = lax.optimization_barrier(
        jnp.stack(
            [
                grad_gain_one,
                grad_gain_two,
                grad_gain_three,
                grad_bias_one,
                grad_bias_two,
                grad_bias_three,
            ]
        )
    )
    drive.add(
        "S1",
        cube.scatter(
            [(token_turned[0], jnp.concatenate([self_dq, self_dk], axis=1))], orders[SCATTER["S1"]]
        ),
    )
    drive.add(
        "S2",
        cube.scatter(
            [(token_turned[1], self_dv), (self_mixed_turned, self_branch)],
            orders[SCATTER["S2"]],
            cube.columns(grad_norms, orders[SCATTER["S2"]]),
        ),
    )
    drive.advance(STEPS["tail"])
    drive.finish(["N", "W", "P1", "P2", "S1", "S2"])
    sums = drive.results
    grad_norms = sums["S2"][:, 2 * width : 2 * width + 6].T
    widen_mine, widen_other = sums["W"]
    grad_widen = jnp.stack(
        [
            block.reshape(own, far, hidden_width // (2 * far))
            for block in both_sides(widen_mine, widen_other)
        ],
        axis=2,
    ).reshape(own, hidden_width)
    return (
        layer_out[None],
        grad_tokens[None],
        grad_memory[None],
        jnp.stack([sums["S1"][:, :width], sums["S1"][:, width:], sums["S2"][:, :width]]),
        sums["S2"][:, width : 2 * width],
        jnp.stack([sums["P2"][:, :width], sums["P1"][:, :width], sums["P1"][:, width:]]),
        sums["P2"][:, width:],
        grad_widen,
        sums["N"],
        grad_norms[:3],
        grad_norms[3:],
    )


def solution(mesh):
    cube = Cube(mesh)
    return jax.shard_map(
        functools.partial(per_device, cube),
        mesh=cube.mesh,
        in_specs=(
            P(AXES, None, None),
            P(AXES, None, None),
            P(AXES, None),
            P(AXES, None),
            P(AXES, None),
            P(None, AXES, None),
            P(AXES, None),
            P(None, AXES, None),
            P(AXES, None),
            P(AXES, None),
            P(AXES, None),
            P(None, AXES),
            P(None, AXES),
            P(AXES, None, None),
        ),
        out_specs=(
            P(AXES, None, None),
            P(AXES, None, None),
            P(AXES, None, None),
            P(None, AXES, None),
            P(AXES, None),
            P(None, AXES, None),
            P(AXES, None),
            P(AXES, None),
            P(AXES, None),
            P(None, AXES),
            P(None, AXES),
        ),
        check_vma=False,
    )
```

time: 2190 us -> 436 us (0.20)
  waiting for transfers between devices: 1830 us -> 137 us
  blocking collectives: 134 us -> 0 us
  starting transfers between devices: 0.94 us -> 59.5 us
  matrix products: 116 us -> 83.8 us
    unnamed x16 -> x2, waiting for transfers between devices: 874 us -> 0.03 us
    reduce_scatter x2 -> x0, waiting for transfers between devices: 714 us -> none  [the longest x1 360 us: per_device(): lax.psum_scatter(product(second_low.T, grad_hidden), ('dp', 'fsdp'), scat...]
    all_gather x6 -> x2, waiting for transfers between devices: 240 us -> 0.01 us  [the longest x1 0.01 us: gather_widen(): lax.all_gather(drive.after(widen_shard), ('far', 'core', 'fsdp'), axis=1,...]
    ppermute x0 -> x54, waiting for transfers between devices: none -> 136 us  [swap(): lax.ppermute(block, axis, [(i, i ^ 1 << k) for i in range(self.sizes[axis...]
    all_gather x2 -> x0, blocking collectives: 134 us -> none  [the longest x1 70.4 us: per_device(): lax.all_gather(norm_gain, ('dp', 'fsdp'), axis=1, tiled=True)]
    ppermute x0 -> x54, starting transfers between devices: none -> 59.1 us  [swap(): lax.ppermute(block, axis, [(i, i ^ 1 << k) for i in range(self.sizes[axis...]
    dot_general x27 -> x48, matrix products: 101 us -> 69.3 us  [product(): return jnp.dot(first_side, other_side, preferred_element_type=jnp.float32)]
    unnamed x92 -> x336, local copies, waits for them, and re-layouts: 48.4 us -> 38.4 us
  transfers between devices with their start and end apart: 12 -> 56, of which waited for: 10 -> 26; matrix products, arithmetic and copies ran while one was open for 7% -> 33% of each run, Pallas kernels for 0% -> 4%
where the time goes in v2:
time: 436 us; the launch traced here: 432 us
  waiting for transfers between devices  137 us (31%)
  matrix products  83.8 us (19%)
  local copies, waits for them, and re-layouts  70.6 us (16%)
  starting transfers between devices  59.5 us (14%)
  other arithmetic  45.6 us (10%)
  Pallas kernels  18.9 us (4%)
  between operations  16.6 us (4%)
    ppermute x54, waiting for transfers between devices, swap(): lax.ppermute(block, axis, [(i, i ^ 1 << k) for i in range(self.sizes[axis...  136 us
    dot_general x48, matrix products, product(): return jnp.dot(first_side, other_side, preferred_element_type=jnp.float32)  69.3 us
    ppermute x54, starting transfers between devices, swap(): lax.ppermute(block, axis, [(i, i ^ 1 << k) for i in range(self.sizes[axis...  59.1 us
    unnamed x336, local copies, waits for them, and re-layouts  38.4 us
    pallas_call x4, Pallas kernels, natural(): pl.pallas_call(body, out_shape=[jax.ShapeDtypeStruct((count, rows, column...  15.6 us
    concatenate x12, other arithmetic, gather(): held = jnp.concatenate([held, (yield (held, bit))], axis=0)  10.1 us
    add x8, other arithmetic, scatter(): kept = kept[:middle] + got[:middle].astype(jnp.float32)  9.15 us
  transfers between devices with their start and end apart: 56, of which 26 were waited for; matrix products, arithmetic and copies ran while one was open for 33% of the time, Pallas kernels for 4%

profile of v2, /device:TPU:0, one launch (start us, length us, event | category | flops | bytes accessed | tf_op | source)
XLA Modules:
  0.0 431.6 jit_solution(10323166769822990281)
XLA Ops:
  9.7 4.1 collective-permute-start
  18.5 8.6 %collective-permute-done.1 = bf16[1,64,1024]{2,1,0:T(8,128)(2,1)S(1)} collective-permute-done((bf16[1,64,1024]{2,1,0:T(8,128)(2,1)S(1)}, bf16[1,64,1024]{2,1,0:T(8,128)(2,1)S(1)}, u32[]{:S(2)}, u32[]{:S(2)}) %collective-permute-start.1) | collective-permute-done | bytes 131104 | tf_op jit(solution)/shard_map/ppermute | solution.py:148
  31.6 7.7 %collective-permute-done.3 = bf16[2,64,1024]{2,1,0:T(8,128)(2,1)S(1)} collective-permute-done((bf16[2,64,1024]{2,1,0:T(8,128)(2,1)S(1)}, bf16[2,64,1024]{2,1,0:T(8,128)(2,1)S(1)}, u32[]{:S(2)}, u32[]{:S(2)}) %collective-permute-start.3) | collective-permute-done | bytes 262176 | tf_op jit(solution)/shard_map/ppermute | solution.py:148
  41.7 2.9 collective-permute-done.2
  47.8 2.7 collective-permute-start.6
  51.2 5.1 %collective-permute-done.6 = bf16[1,64,1024]{2,1,0:T(8,128)(2,1)S(1)} collective-permute-done((bf16[1,64,1024]{2,1,0:T(8,128)(2,1)S(1)}, bf16[1,64,1024]{2,1,0:T(8,128)(2,1)S(1)}, u32[]{:S(2)}, u32[]{:S(2)}) %collective-permute-start.6) | collective-permute-done | bytes 131104 | tf_op jit(solution)/shard_map/ppermute | solution.py:148
  62.0 3.2 collective-permute-done.12
  74.2 20.8 %collective-permute-done.10 = bf16[8,64,1024]{2,1,0:T(8,128)(2,1)S(1)} collective-permute-done((bf16[8,64,1024]{2,1,0:T(8,128)(2,1)}, bf16[8,64,1024]{2,1,0:T(8,128)(2,1)S(1)}, u32[]{:S(2)}, u32[]{:S(2)}) %collective-permute-start.10) | collective-permute-done | bytes 1048608 | tf_op jit(solution)/shard_map/ppermute | solution.py:148
  107.3 6.4 %collective-permute-done.15 = bf16[4,64,1024]{2,1,0:T(8,128)(2,1)} collective-permute-done((bf16[4,64,1024]{2,1,0:T(8,128)(2,1)}, bf16[4,64,1024]{2,1,0:T(8,128)(2,1)}, u32[]{:S(2)}, u32[]{:S(2)}) %collective-permute-start.15) | collective-permute-done | bytes 524320 | tf_op jit(solution)/shard_map/ppermute | solution.py:148
  115.8 8.2 %collective-permute-done.14 = bf16[4,64,1024]{2,1,0:T(8,128)(2,1)S(1)} collective-permute-done((bf16[4,64,1024]{2,1,0:T(8,128)(2,1)}, bf16[4,64,1024]{2,1,0:T(8,128)(2,1)S(1)}, u32[]{:S(2)}, u32[]{:S(2)}) %collective-permute-start.14) | collective-permute-done | bytes 524320 | tf_op jit(solution)/shard_map/ppermute | solution.py:148
  130.7 2.8 natural_order.5
  137.8 6.0 %natural_order.4 = (bf16[32,32,1024]{2,1,0:T(8,128)(2,1)S(1)}, bf16[32,32,1024]{2,1,0:T(8,128)(2,1)S(1)}, bf16[32,16,1024]{2,1,0:T(8,128)(2,1)S(1)}) custom-call(s32[1]{0:T(128)} %bitcast.1.index_ref, bf16[16,80,1024]{2,1,0:T(8,128)(2,1)S(1)} %constant_dynamic-update-slice_fusion.5.low_ref, bf16[16,80,1024]{2,1,0:T(8,128)(2,1)} %collective-permute-done.13.high_ref), custom_call_target="tpu_custom_call" | custom-call | tf_op jit(solution)/shard_map/natural_order/pallas_call | solution.py:194
  148.5 3.9 collective-permute-done.18
  164.2 2.9 natural_order.6
  172.8 3.9 natural_order.7
  180.9 2.6 convolution_convert_fusion.10
  202.1 4.2 collective-permute-done.21.refs_1_
  206.3 5.6 %multiply_convert_fusion.2 = (bf16[256,2048]{1,0:T(8,128)(2,1)}, f32[256,2048]{1,0:T(8,128)}) fusion(bf16[256,1024]{1,0:T(8,128)(2,1)} %collective-permute-done.21.refs_1_, bf16[1024,2048]{1,0:T(8,128)(2,1)} %bitcast.387), kind=kOutput, calls=%fused_computation.57 | convolution fusion | flops 1078460416 | bytes 7864320 | tf_op jit(solution)/shard_map/dot_general | solution.py:25
  211.9 3.9 convolution_convert_fusion.17
  218.7 3.0 multiply_convert_fusion.3
  222.5 6.5 %collective-permute-done.22 = bf16[256,1024]{1,0:T(8,128)(2,1)S(1)} collective-permute-done((bf16[256,1024]{1,0:T(8,128)(2,1)S(1)}, bf16[256,1024]{1,0:T(8,128)(2,1)S(1)}, u32[]{:S(2)}, u32[]{:S(2)}) %collective-permute-start.22) | collective-permute-done | bytes 524320 | tf_op jit(solution)/shard_map/ppermute | solution.py:148
  236.6 9.1 %collective-permute-done.23 = bf16[256,1024]{1,0:T(8,128)(2,1)S(1)} collective-permute-done((bf16[256,1024]{1,0:T(8,128)(2,1)S(1)}, bf16[256,1024]{1,0:T(8,128)(2,1)S(1)}, u32[]{:S(2)}, u32[]{:S(2)}) %collective-permute-start.23) | collective-permute-done | bytes 524320 | tf_op jit(solution)/shard_map/ppermute | solution.py:148
  256.3 4.3 %collective-permute-done.24 = bf16[256,1024]{1,0:T(8,128)(2,1)S(1)} collective-permute-done((bf16[256,1024]{1,0:T(8,128)(2,1)S(1)}, bf16[256,1024]{1,0:T(8,128)(2,1)S(1)}, u32[]{:S(2)}, u32[]{:S(2)}) %collective-permute-start.24) | collective-permute-done | bytes 524320 | tf_op jit(solution)/shard_map/ppermute | solution.py:148
  272.1 3.7 multiply_reduce_fusion.1
  296.6 2.7 slice_add_fusion.4
  299.3 2.8 slice_add_fusion.5
  306.0 3.4 multiply_reduce_fusion
  360.5 21.1 %collective-permute-done.35 = bf16[256,2048]{1,0:T(8,128)(2,1)S(1)} collective-permute-done((bf16[256,2048]{1,0:T(8,128)(2,1)S(1)}, bf16[256,2048]{1,0:T(8,128)(2,1)S(1)}, u32[]{:S(2)}, u32[]{:S(2)}) %collective-permute-start.35) | collective-permute-done | bytes 1048608 | tf_op jit(solution)/shard_map/ppermute | solution.py:148
  394.4 3.3 collective-permute-done.46
  398.3 3.6 collective-permute-start.51
  404.3 2.7 collective-permute-done.44
  413.1 6.9 %collective-permute-done.48 = bf16[32,2048]{1,0:T(8,128)(2,1)S(1)} collective-permute-done((bf16[32,2048]{1,0:T(8,128)(2,1)S(1)}, bf16[32,2048]{1,0:T(8,128)(2,1)S(1)}, u32[]{:S(2)}, u32[]{:S(2)}) %collective-permute-start.48) | collective-permute-done | bytes 131104 | tf_op jit(solution)/shard_map/ppermute | solution.py:148
  (637 shorter events, 236.4 us)
Async XLA Ops:
  7.2 199.1 %all-gather.3.cloned.1.call-start = ((), (), s32[]{:S(2)}) async-start(), calls=%async_computation | async-start | bytes 4456448 | tf_op jit(solution)/shard_map/all_gather | solution.py:392
  9.7 18.2 %collective-permute-start = (bf16[1,80,1024]{2,1,0:T(8,128)(2,1)S(1)}, bf16[1,80,1024]{2,1,0:T(8,128)(2,1)S(1)}, u32[]{:S(2)}, u32[]{:S(2)}) collective-permute-start(bf16[1,80,1024]{2,1,0:T(8,128)(2,1)S(1)} %maximum_bitcast_fusion), channel_id=1, source_target_pairs={{0,4},{1,5},{2,6},{3,7},{4,0},{5,1},{6,2},{7,3},{8,12},{9,13},{10,... | collective-permute-start | bytes 491528 | tf_op jit(solution)/shard_map/ppermute | solution.py:148
  16.6 30.1 %collective-permute-start.8 = (bf16[32,2048]{1,0:T(8,128)(2,1)S(1)}, bf16[32,2048]{1,0:T(8,128)(2,1)}, u32[]{:S(2)}, u32[]{:S(2)}) collective-permute-start(bf16[32,2048]{1,0:T(8,128)(2,1)S(1)} %bitcast.373), channel_id=1, source_target_pairs={{0,16},{16,0},{1,17},{17,1},{2,18},{18,2},{3,19},{19,3},{4,20},{20... | collective-permute-start | bytes 393224 | tf_op jit(solution)/shard_map/ppermute | solution.py:148
  28.0 16.6 %collective-permute-start.2 = (bf16[2,80,1024]{2,1,0:T(8,128)(2,1)S(1)}, bf16[2,80,1024]{2,1,0:T(8,128)(2,1)S(1)}, u32[]{:S(2)}, u32[]{:S(2)}) collective-permute-start(bf16[2,80,1024]{2,1,0:T(8,128)(2,1)S(1)} %pad_maximum_fusion.28), channel_id=1, source_target_pairs={{0,2},{1,3},{2,0},{3,1},{4,6},{5,7},{6,4},{7,5},{8,10},{9,11},{10,... | collective-permute-start | bytes 983048 | tf_op jit(solution)/shard_map/ppermute | solution.py:148
  29.5 21.7 %collective-permute-start.7 = (bf16[1,64,1024]{2,1,0:T(8,128)(2,1)S(1)}, bf16[1,64,1024]{2,1,0:T(8,128)(2,1)S(1)}, u32[]{:S(2)}, u32[]{:S(2)}) collective-permute-start(bf16[1,64,1024]{2,1,0:T(8,128)(2,1)S(1)} %bitcast.328), channel_id=1, source_target_pairs={{0,4},{1,5},{2,6},{3,7},{4,0},{5,1},{6,2},{7,3},{8,12},{9,13},{10,... | collective-permute-start | bytes 393224 | tf_op jit(solution)/shard_map/ppermute | solution.py:148
  40.2 18.3 %collective-permute-start.5 = (bf16[4,64,1024]{2,1,0:T(8,128)(2,1)}, bf16[4,64,1024]{2,1,0:T(8,128)(2,1)S(1)}, u32[]{:S(2)}, u32[]{:S(2)}) collective-permute-start(bf16[4,64,1024]{2,1,0:T(8,128)(2,1)} %pad_maximum_fusion.22), channel_id=1, source_target_pairs={{0,16},{16,0},{1,17},{17,1},{2,18},{18,2},{3,19},{19,3},{4,20},{20... | collective-permute-start | bytes 1572872 | tf_op jit(solution)/shard_map/ppermute | solution.py:148
  45.5 15.2 %collective-permute-start.4 = (bf16[4,80,1024]{2,1,0:T(8,128)(2,1)}, bf16[4,80,1024]{2,1,0:T(8,128)(2,1)S(1)}, u32[]{:S(2)}, u32[]{:S(2)}) collective-permute-start(bf16[4,80,1024]{2,1,0:T(8,128)(2,1)} %pad_maximum_fusion.14), channel_id=1, source_target_pairs={{0,1},{1,0},{2,3},{3,2},{4,5},{5,4},{6,7},{7,6},{8,9},{9,8},{10,11... | collective-permute-start | bytes 1966088 | tf_op jit(solution)/shard_map/ppermute | solution.py:148
  68.8 143.0 %all-gather.5.cloned.1.call-start = ((), (), s32[]{:S(2)}) async-start(), calls=%async_computation.1 | async-start | bytes 4456448 | tf_op jit(solution)/shard_map/all_gather | solution.py:400
  69.2 25.8 %collective-permute-start.10 = (bf16[8,64,1024]{2,1,0:T(8,128)(2,1)}, bf16[8,64,1024]{2,1,0:T(8,128)(2,1)S(1)}, u32[]{:S(2)}, u32[]{:S(2)}) collective-permute-start(bf16[8,64,1024]{2,1,0:T(8,128)(2,1)} %pad_maximum_fusion.7), channel_id=1, source_target_pairs={{0,1},{1,0},{2,3},{3,2},{4,5},{5,4},{6,7},{7,6},{8,9},{9,8},{10,11... | collective-permute-start | bytes 3145736 | tf_op jit(solution)/shard_map/ppermute | solution.py:148
  69.8 28.2 %collective-permute-start.9 = (bf16[8,80,1024]{2,1,0:T(8,128)(2,1)}, bf16[8,80,1024]{2,1,0:T(8,128)(2,1)S(1)}, u32[]{:S(2)}, u32[]{:S(2)}) collective-permute-start(bf16[8,80,1024]{2,1,0:T(8,128)(2,1)} %pad_maximum_fusion.4), channel_id=1, source_target_pairs={{0,16},{16,0},{1,17},{17,1},{2,18},{18,2},{3,19},{19,3},{4,20},{20... | collective-permute-start | bytes 3932168 | tf_op jit(solution)/shard_map/ppermute | solution.py:148
  96.0 34.7 %collective-permute-start.16 = (bf16[16,64,1024]{2,1,0:T(8,128)(2,1)}, bf16[16,64,1024]{2,1,0:T(8,128)(2,1)}, u32[]{:S(2)}, u32[]{:S(2)}) collective-permute-start(bf16[16,64,1024]{2,1,0:T(8,128)(2,1)} %constant_dynamic-update-slice_fusion.low_ref), channel_id=1, source_target_pairs={{0,8},{8,0},{1,9},{9,1},{2,10},{10,2},{3,11},{11,3},{4,12},{12,4},... | collective-permute-start | bytes 6291464 | tf_op jit(solution)/shard_map/ppermute | solution.py:148
  98.1 39.6 %collective-permute-start.13 = (bf16[16,80,1024]{2,1,0:T(8,128)(2,1)S(1)}, bf16[16,80,1024]{2,1,0:T(8,128)(2,1)}, u32[]{:S(2)}, u32[]{:S(2)}) collective-permute-start(bf16[16,80,1024]{2,1,0:T(8,128)(2,1)S(1)} %constant_dynamic-update-slice_fusion.5.low_ref), channel_id=1, source_target_pairs={{0,8},{8,0},{1,9},{9,1},{2,10},{10,2},{3,11},{11,3},{4,12},{12,4},... | collective-permute-start | bytes 7864328 | tf_op jit(solution)/shard_map/ppermute | solution.py:148
  99.1 14.6 %collective-permute-start.15 = (bf16[4,64,1024]{2,1,0:T(8,128)(2,1)}, bf16[4,64,1024]{2,1,0:T(8,128)(2,1)}, u32[]{:S(2)}, u32[]{:S(2)}) collective-permute-start(bf16[4,64,1024]{2,1,0:T(8,128)(2,1)} %pad_maximum_fusion.23), channel_id=1, source_target_pairs={{0,16},{16,0},{1,17},{17,1},{2,18},{18,2},{3,19},{19,3},{4,20},{20... | collective-permute-start | bytes 1572872 | tf_op jit(solution)/shard_map/ppermute | solution.py:148
  101.2 22.8 %collective-permute-start.14 = (bf16[4,64,1024]{2,1,0:T(8,128)(2,1)}, bf16[4,64,1024]{2,1,0:T(8,128)(2,1)S(1)}, u32[]{:S(2)}, u32[]{:S(2)}) collective-permute-start(bf16[4,64,1024]{2,1,0:T(8,128)(2,1)} %pad_maximum_fusion.24), channel_id=1, source_target_pairs={{0,1},{1,0},{2,3},{3,2},{4,5},{5,4},{6,7},{7,6},{8,9},{9,8},{10,11... | collective-permute-start | bytes 1572872 | tf_op jit(solution)/shard_map/ppermute | solution.py:148
  126.0 28.7 %collective-permute-start.17 = (bf16[8,64,1024]{2,1,0:T(8,128)(2,1)}, bf16[8,64,1024]{2,1,0:T(8,128)(2,1)}, u32[]{:S(2)}, u32[]{:S(2)}) collective-permute-start(bf16[8,64,1024]{2,1,0:T(8,128)(2,1)} %pad_maximum_fusion.9), channel_id=1, source_target_pairs={{0,16},{16,0},{1,17},{17,1},{2,18},{18,2},{3,19},{19,3},{4,20},{20... | collective-permute-start | bytes 3145736 | tf_op jit(solution)/shard_map/ppermute | solution.py:148
  127.4 24.9 %collective-permute-start.18 = (bf16[8,64,1024]{2,1,0:T(8,128)(2,1)}, bf16[8,64,1024]{2,1,0:T(8,128)(2,1)}, u32[]{:S(2)}, u32[]{:S(2)}) collective-permute-start(bf16[8,64,1024]{2,1,0:T(8,128)(2,1)} %pad_maximum_fusion.8), channel_id=1, source_target_pairs={{0,1},{1,0},{2,3},{3,2},{4,5},{5,4},{6,7},{7,6},{8,9},{9,8},{10,11... | collective-permute-start | bytes 3145736 | tf_op jit(solution)/shard_map/ppermute | solution.py:148
  266.2 33.0 %collective-permute-start.27 = (bf16[512,1024]{1,0:T(8,128)(2,1)}, bf16[512,1024]{1,0:T(8,128)(2,1)}, u32[]{:S(2)}, u32[]{:S(2)}) collective-permute-start(bf16[512,1024]{1,0:T(8,128)(2,1)} %add_convert_fusion.2), channel_id=1, source_target_pairs={{0,1},{1,0},{2,3},{3,2},{4,5},{5,4},{6,7},{7,6},{8,9},{9,8},{10,11... | collective-permute-start | bytes 3145736 | tf_op jit(solution)/shard_map/ppermute | solution.py:148
  267.0 29.6 %collective-permute-start.28 = (bf16[256,2048]{1,0:T(8,128)(2,1)}, bf16[256,2048]{1,0:T(8,128)(2,1)}, u32[]{:S(2)}, u32[]{:S(2)}) collective-permute-start(bf16[256,2048]{1,0:T(8,128)(2,1)} %add_convert_fusion.3), channel_id=1, source_target_pairs={{0,2},{1,3},{2,0},{3,1},{4,6},{5,7},{6,4},{7,5},{8,10},{9,11},{10,... | collective-permute-start | bytes 3145736 | tf_op jit(solution)/shard_map/ppermute | solution.py:148
  313.1 28.1 %collective-permute-start.32 = (bf16[256,2048]{1,0:T(8,128)(2,1)}, bf16[256,2048]{1,0:T(8,128)(2,1)}, u32[]{:S(2)}, u32[]{:S(2)}) collective-permute-start(bf16[256,2048]{1,0:T(8,128)(2,1)} %add_convert_fusion.1), channel_id=1, source_target_pairs={{0,16},{16,0},{1,17},{17,1},{2,18},{18,2},{3,19},{19,3},{4,20},{20... | collective-permute-start | bytes 3145736 | tf_op jit(solution)/shard_map/ppermute | solution.py:148
  313.5 25.1 %collective-permute-start.33 = (bf16[256,2048]{1,0:T(8,128)(2,1)}, bf16[256,2048]{1,0:T(8,128)(2,1)}, u32[]{:S(2)}, u32[]{:S(2)}) collective-permute-start(bf16[256,2048]{1,0:T(8,128)(2,1)} %pad_maximum_fusion.12), channel_id=1, source_target_pairs={{0,2},{1,3},{2,0},{3,1},{4,6},{5,7},{6,4},{7,5},{8,10},{9,11},{10,... | collective-permute-start | bytes 3145736 | tf_op jit(solution)/shard_map/ppermute | solution.py:148
  314.1 33.1 %collective-permute-start.34 = (bf16[128,2048]{1,0:T(8,128)(2,1)}, bf16[128,2048]{1,0:T(8,128)(2,1)}, u32[]{:S(2)}, u32[]{:S(2)}) collective-permute-start(bf16[128,2048]{1,0:T(8,128)(2,1)} %get-tuple-element.273), channel_id=1, source_target_pairs={{0,1},{1,0},{2,3},{3,2},{4,5},{5,4},{6,7},{7,6},{8,9},{9,8},{10,11... | collective-permute-start | bytes 1572872 | tf_op jit(solution)/shard_map/ppermute | solution.py:148
  322.7 27.3 %collective-permute-start.38 = (bf16[512,2176]{1,0:T(8,128)(2,1)}, bf16[512,2176]{1,0:T(8,128)(2,1)}, u32[]{:S(2)}, u32[]{:S(2)}) collective-permute-start(bf16[512,2176]{1,0:T(8,128)(2,1)} %pad_maximum_fusion), channel_id=1, source_target_pairs={{0,8},{8,0},{1,9},{9,1},{2,10},{10,2},{3,11},{11,3},{4,12},{12,4},... | collective-permute-start | bytes 6684680 | tf_op jit(solution)/shard_map/ppermute | solution.py:148
  325.0 19.3 %collective-permute-start.31 = (bf16[512,2048]{1,0:T(8,128)(2,1)}, bf16[512,2048]{1,0:T(8,128)(2,1)}, u32[]{:S(2)}, u32[]{:S(2)}) collective-permute-start(bf16[512,2048]{1,0:T(8,128)(2,1)} %convolution_convert_fusion), channel_id=1, source_target_pairs={{0,8},{8,0},{1,9},{9,1},{2,10},{10,2},{3,11},{11,3},{4,12},{12,4},... | collective-permute-start | bytes 6291464 | tf_op jit(solution)/shard_map/ppermute | solution.py:148
  338.7 16.8 %collective-permute-start.37 = (bf16[256,1024]{1,0:T(8,128)(2,1)S(1)}, bf16[256,1024]{1,0:T(8,128)(2,1)S(1)}, u32[]{:S(2)}, u32[]{:S(2)}) collective-permute-start(bf16[256,1024]{1,0:T(8,128)(2,1)S(1)} %copy-done.83), channel_id=1, source_target_pairs={{0,2},{1,3},{2,0},{3,1},{4,6},{5,7},{6,4},{7,5},{8,10},{9,11},{10,... | collective-permute-start | bytes 1572872 | tf_op jit(solution)/shard_map/ppermute | solution.py:148
  341.3 16.8 %collective-permute-start.36 = (bf16[128,2048]{1,0:T(8,128)(2,1)S(1)}, bf16[128,2048]{1,0:T(8,128)(2,1)S(1)}, u32[]{:S(2)}, u32[]{:S(2)}) collective-permute-start(bf16[128,2048]{1,0:T(8,128)(2,1)S(1)} %get-tuple-element.171), channel_id=1, source_target_pairs={{0,16},{16,0},{1,17},{17,1},{2,18},{18,2},{3,19},{19,3},{4,20},{20... | collective-permute-start | bytes 1572872 | tf_op jit(solution)/shard_map/ppermute | solution.py:148
  344.2 14.9 %collective-permute-start.40 = (bf16[128,2048]{1,0:T(8,128)(2,1)S(1)}, bf16[128,2048]{1,0:T(8,128)(2,1)S(1)}, u32[]{:S(2)}, u32[]{:S(2)}) collective-permute-start(bf16[128,2048]{1,0:T(8,128)(2,1)S(1)} %get-tuple-element.180), channel_id=1, source_target_pairs={{0,1},{1,0},{2,3},{3,2},{4,5},{5,4},{6,7},{7,6},{8,9},{9,8},{10,11... | collective-permute-start | bytes 1572872 | tf_op jit(solution)/shard_map/ppermute | solution.py:148
  347.2 34.4 %collective-permute-start.35 = (bf16[256,2048]{1,0:T(8,128)(2,1)S(1)}, bf16[256,2048]{1,0:T(8,128)(2,1)S(1)}, u32[]{:S(2)}, u32[]{:S(2)}) collective-permute-start(bf16[256,2048]{1,0:T(8,128)(2,1)S(1)} %add_convert_fusion), channel_id=1, source_target_pairs={{0,1},{1,0},{2,3},{3,2},{4,5},{5,4},{6,7},{7,6},{8,9},{9,8},{10,11... | collective-permute-start | bytes 3145736 | tf_op jit(solution)/shard_map/ppermute | solution.py:148
  353.3 29.3 %collective-permute-start.43 = (bf16[256,2176]{1,0:T(8,128)(2,1)S(1)}, bf16[256,2176]{1,0:T(8,128)(2,1)S(1)}, u32[]{:S(2)}, u32[]{:S(2)}) collective-permute-start(bf16[256,2176]{1,0:T(8,128)(2,1)S(1)} %pad_maximum_fusion.5), channel_id=1, source_target_pairs={{0,16},{16,0},{1,17},{17,1},{2,18},{18,2},{3,19},{19,3},{4,20},{20... | collective-permute-start | bytes 3342344 | tf_op jit(solution)/shard_map/ppermute | solution.py:148
  355.5 28.6 %collective-permute-start.42 = (bf16[64,2048]{1,0:T(8,128)(2,1)S(1)}, bf16[64,2048]{1,0:T(8,128)(2,1)S(1)}, u32[]{:S(2)}, u32[]{:S(2)}) collective-permute-start(bf16[64,2048]{1,0:T(8,128)(2,1)S(1)} %fusion.67), channel_id=1, source_target_pairs={{0,4},{1,5},{2,6},{3,7},{4,0},{5,1},{6,2},{7,3},{8,12},{9,13},{10,... | collective-permute-start | bytes 786440 | tf_op jit(solution)/shard_map/ppermute | solution.py:148
  358.0 33.0 %collective-permute-start.50 = (bf16[128,1024]{1,0:T(8,128)(2,1)S(1)}, bf16[128,1024]{1,0:T(8,128)(2,1)S(1)}, u32[]{:S(2)}, u32[]{:S(2)}) collective-permute-start(bf16[128,1024]{1,0:T(8,128)(2,1)S(1)} %fusion.68), channel_id=1, source_target_pairs={{0,4},{1,5},{2,6},{3,7},{4,0},{5,1},{6,2},{7,3},{8,12},{9,13},{10,... | collective-permute-start | bytes 786440 | tf_op jit(solution)/shard_map/ppermute | solution.py:148
  359.2 28.1 %collective-permute-start.41 = (bf16[64,2048]{1,0:T(8,128)(2,1)S(1)}, bf16[64,2048]{1,0:T(8,128)(2,1)S(1)}, u32[]{:S(2)}, u32[]{:S(2)}) collective-permute-start(bf16[64,2048]{1,0:T(8,128)(2,1)S(1)} %get-tuple-element.181), channel_id=1, source_target_pairs={{0,1},{1,0},{2,3},{3,2},{4,5},{5,4},{6,7},{7,6},{8,9},{9,8},{10,11... | collective-permute-start | bytes 786440 | tf_op jit(solution)/shard_map/ppermute | solution.py:148
  382.8 14.8 %collective-permute-start.46 = (bf16[128,2176]{1,0:T(8,128)(2,1)S(1)}, bf16[128,2176]{1,0:T(8,128)(2,1)S(1)}, u32[]{:S(2)}, u32[]{:S(2)}) collective-permute-start(bf16[128,2176]{1,0:T(8,128)(2,1)S(1)} %get-tuple-element.190), channel_id=1, source_target_pairs={{0,1},{1,0},{2,3},{3,2},{4,5},{5,4},{6,7},{7,6},{8,9},{9,8},{10,11... | collective-permute-start | bytes 1671176 | tf_op jit(solution)/shard_map/ppermute | solution.py:148
  (187 other events, 1271.1 us)
Sparse Core Ops, SparseCore 0:
  69.0 60.8 all-gather.2
  157.1 49.7 all-gather.4

commit v3 on v2

--- a/solution.py
+++ b/solution.py
@@ -33,13 +33,13 @@
 GATHER = {"s1": "A", "s2": "B", "c1": "A", "c2": "B"}
 SCATTER = {"N": "E", "W": "F", "P1": "B", "P2": "D", "S1": "A", "S2": "B"}
 STEPS = {
-    "start": [],
-    "early": ["s1", "s2", "s1", "s2"],
-    "self": ["c1", "c2", "s1", "s2", "c1", "c2", "widen", "s1", "s2", "c1", "c2", "s1", "s2"],
-    "cross": ["c1", "c2", "narrow", "c1", "c2"],
     "gs": ["W", "N"],
     "gf": ["P2", "P1", "W", "N"],
-    "tail": ["P2", "P1", "S1", "S2", "W", "N", "P2", "S1", "S2", "W", "N", "P1", "P2", "S1", "S2", "W", "P1", "P2", "S1", "S2", "P1", "S1", "S2"],
+    "pre": [],
+    "tail": ["P2", "P1", "S1", "S2", "W", "N", "P2", "P1", "S1", "S2", "W", "N", "P2", "P1", "S2", "S1", "W", "P2", "P1", "S2", "S1", "S2", "S1"],
+    "early": ["s", "cross", "s", "c", "s", "s1", "s2", "c"],
+    "self": ["s1", "s2", "c", "wide", "c1", "c2", "s1", "s2", "c1", "c2", "s1", "s2"],
+    "cross": ["c1", "c2", "c1", "c2"],
 }
 
 
@@ -138,6 +138,7 @@
             "D": [CORE, close[1], PAIR, close[0], *close[2:], *apart],
             "E": [CORE, *close, *apart],
             "F": [CORE, close[1], close[0], *close[2:], *apart],
+            "H": [CORE, *close[1:], close[0], *apart],
         }
 
     def index(self, place):
@@ -154,21 +155,26 @@
             for p in range(1 << len(order))
         ]
 
-    def gather(self, shard, order):
-        held = shard[None]
-        for bit in order[:0:-1]:
+    def spread(self, held, bits):
+        for bit in bits:
             held = jnp.concatenate([held, (yield held, bit)], axis=0)
+        return held
+
+    def gather(self, held, order):
+        done = held.shape[0].bit_length() - 1
+        held = yield from self.spread(held, order[:0:-1][done:])
         return held, (yield held, order[0])
 
-    def natural(self, halves, order, segments):
+    def natural(self, halves, order, segments, place):
         low, high = halves
-        offsets = self.offsets(order, self.place)
-        count, half = self.count, self.count // 2
+        offsets = self.offsets(order, place)
+        count, half = 2 * low.shape[0], low.shape[0]
         columns = low.shape[2]
         starts = [sum(segments[:k]) for k in range(len(segments))]
+        index = self.index(place)
         if any(rows % 16 for rows in segments):
             where = np.argsort(np.array(offsets))
-            picked = jnp.asarray(where)[jnp.arange(count) ^ self.index(self.place)]
+            picked = jnp.asarray(where)[jnp.arange(count) ^ index]
             blocks = jnp.take(jnp.concatenate(halves, axis=0), picked, axis=0)
             return [
                 blocks[:, start : start + rows].reshape(count * rows, columns)
@@ -203,8 +209,50 @@
             scratch_shapes=[pltpu.SemaphoreType.DMA((count, len(segments)))],
             compiler_params=pltpu.CompilerParams(vmem_limit_bytes=40 * 2**20),
             name="natural_order",
-        )(self.index(self.place).astype(jnp.int32).reshape(1), low, high)
+        )(index.astype(jnp.int32).reshape(1), low, high)
         return [block.reshape(count * rows, columns) for block, rows in zip(moved, segments)]
+
+    def unpacked(self, packed):
+        rows, columns = packed.shape[1] // (self.count // 2), packed.shape[2]
+        count, far, half = self.count // 2, self.far, columns // 2
+
+        def widen(blocks):
+            return blocks.reshape(2, far, -1, columns).transpose(1, 0, 2, 3).reshape(-1, columns)
+
+        if rows % 16:
+            narrow = packed[2:].reshape(2, count, rows, 2, half).transpose(1, 3, 0, 2, 4)
+            return widen(packed[:2]), narrow.reshape(-1, half)
+
+        def body(packed_ref, widen_ref, narrow_ref, sems):
+            copies = [pltpu.make_async_copy(packed_ref.at[pl.ds(0, 2)], widen_ref, sems.at[0])]
+            for p in range(count):
+                for k in range(4):
+                    source = packed_ref.at[
+                        2 + k % 2, pl.ds(p * rows, rows), pl.ds((k // 2) * half, half)
+                    ]
+                    copies.append(
+                        pltpu.make_async_copy(
+                            source, narrow_ref.at[p, pl.ds(k * rows, rows)], sems.at[1 + 4 * p + k]
+                        )
+                    )
+            for copy in copies:
+                copy.start()
+            for copy in copies:
+                copy.wait()
+
+        wide, narrow = pl.pallas_call(
+            body,
+            out_shape=[
+                jax.ShapeDtypeStruct((2, count * rows, columns), packed.dtype),
+                jax.ShapeDtypeStruct((count, 4 * rows, half), packed.dtype),
+            ],
+            in_specs=[pl.BlockSpec(memory_space=pl.ANY)],
+            out_specs=[pl.BlockSpec(memory_space=pltpu.VMEM)] * 2,
+            scratch_shapes=[pltpu.SemaphoreType.DMA((1 + 4 * count,))],
+            compiler_params=pltpu.CompilerParams(vmem_limit_bytes=40 * 2**20),
+            name="unpacked",
+        )(packed)
+        return widen(wide), narrow.reshape(-1, half)
 
     def turned(self, sources, orders, place):
         tokens, features = sources[0].shape
@@ -294,7 +342,7 @@
         self.before = {bit: [] for bit in cube.place}
         self.chains, self.got, self.results = {}, {}, {}
         self.token = None
-        self.hooks = {}
+        self.starts, self.calls = {}, {}
 
     def swap(self, block, bit):
         past = self.before[bit]
@@ -320,8 +368,12 @@
 
     def advance(self, names):
         for name in names:
-            if name in self.hooks:
-                self.results[name] = self.hooks.pop(name)()
+            if name in self.calls:
+                self.results[name] = self.calls.pop(name)()
+                continue
+            if name in self.starts:
+                self.add(name, self.starts.pop(name)())
+                continue
             if name in self.results:
                 continue
             got = self.after(self.got[name])
@@ -329,6 +381,7 @@
                 block, bit = self.chains[name].send(got)
             except StopIteration as stop:
                 self.results[name] = stop.value
+                self.token = got
                 continue
             self.token = block
             self.got[name] = self.swap(block, bit)
@@ -386,40 +439,37 @@
         lax.dynamic_index_in_dim(shard, k, axis=2, keepdims=False).reshape(own, hidden_width // 2)
         for k in (side, 1 - side)
     )
-    widen_shard = jnp.stack(both_sides(mine, drive.swap(other, PAIR)))
-
-    def gather_widen():
-        full = lax.all_gather(drive.after(widen_shard), ("far", "core", "fsdp"), axis=1, tiled=True)
-        return (
-            full.reshape(2, far, width // (2 * far), hidden_width // 2)
-            .transpose(1, 0, 2, 3)
-            .reshape(width, hidden_width // 2)
-        )
-
-    def gather_narrow():
-        return lax.all_gather(drive.after(narrow_weight), ("far", "core", "fsdp"), axis=0, tiled=True)
-
-    drive.hooks = {"widen": gather_widen, "narrow": gather_narrow}
-    drive.advance(STEPS["start"])
+    narrow_shard = jnp.concatenate([narrow_weight[: 2 * own], narrow_weight[2 * own :]], axis=1)
+    wide_shard = jnp.concatenate(
+        [*both_sides(mine, drive.swap(other, PAIR)), narrow_shard], axis=0
+    ).reshape(4, own, 2 * width)
+
+    def gather_wide():
+        return lax.all_gather(drive.after(wide_shard), ("far", "core", "fsdp"), axis=1, tiled=True)
+
+    def gather_cross():
+        return lax.all_gather(drive.after(cross_project[1:]), AXES, axis=1, tiled=True)
+
     norm_rows = jnp.concatenate([norm_gain, norm_bias], axis=0)
     norm_rows = jnp.pad(norm_rows, ((0, 16 - 6), (0, width - own)))
-    drive.add("s1", cube.gather(self_project[:2].reshape(2 * own, width), orders[GATHER["s1"]]))
-    drive.add(
-        "s2",
-        cube.gather(
-            jnp.concatenate([self_project[2], self_output, norm_rows], axis=0), orders[GATHER["s2"]]
-        ),
-    )
+    shared = orders["A"][:2:-1]
+    self_shard = jnp.concatenate([self_project.reshape(3 * own, width), self_output, norm_rows], axis=0)
+    cross_shard = jnp.concatenate([cross_project[0], cross_output], axis=0)
+    drive.calls = {"wide": gather_wide, "cross": gather_cross}
+    drive.starts = {
+        "s": lambda: cube.spread(self_shard[None], shared),
+        "c": lambda: cube.spread(cross_shard[None], shared),
+        "s1": lambda: cube.gather(drive.finish(["s"])[0][:, : 2 * own], orders[GATHER["s1"]]),
+        "s2": lambda: cube.gather(drive.finish(["s"])[0][:, 2 * own :], orders[GATHER["s2"]]),
+        "c1": lambda: cube.gather(drive.finish(["c"])[0][:, :own], orders[GATHER["c1"]]),
+        "c2": lambda: cube.gather(drive.finish(["c"])[0][:, own:], orders[GATHER["c2"]]),
+    }
     drive.advance(STEPS["early"])
-    drive.add("c1", cube.gather(cross_project[:2].reshape(2 * own, width), orders[GATHER["c1"]]))
-    drive.add(
-        "c2",
-        cube.gather(jnp.concatenate([cross_project[2], cross_output], axis=0), orders[GATHER["c2"]]),
-    )
+    drive.finish(["s", "c"])
     drive.advance(STEPS["self"])
     drive.finish(["s1", "s2"])
-    query_full, key_full = cube.natural(drive.results["s1"], orders[GATHER["s1"]], [own, own])
-    value_full, self_final, norms = cube.natural(drive.results["s2"], orders[GATHER["s2"]], [own, own, 16])
+    query_full, key_full = cube.natural(drive.results["s1"], orders[GATHER["s1"]], [own, own], cube.place)
+    value_full, self_final, norms = cube.natural(drive.results["s2"], orders[GATHER["s2"]], [own, own, 16], cube.place)
     self_stack = [query_full, key_full, value_full]
     norms = norms.reshape(count, 16, width)[:, :6, :own].transpose(1, 0, 2).reshape(6, width)
     norms = norms.astype(jnp.float32)
@@ -434,15 +484,17 @@
     drive.done(first_low)
     drive.advance(STEPS["cross"])
     drive.finish(["c1", "c2"])
-    widen_full, narrow_full = drive.finish(["widen", "narrow"])
-    query_full, key_full = cube.natural(drive.results["c1"], orders[GATHER["c1"]], [own, own])
-    value_full, cross_final = cube.natural(drive.results["c2"], orders[GATHER["c2"]], [own, own])
-    cross_stack = [query_full, key_full, value_full]
+    drive.finish(["wide", "cross"])
+    (query_full,) = cube.natural(drive.results["c1"], orders[GATHER["c1"]], [own], cube.place)
+    (cross_final,) = cube.natural(drive.results["c2"], orders[GATHER["c2"]], [own], cube.place)
+    cross_stack = [query_full, *drive.results["cross"]]
     cross_query, cross_key, cross_value = project_three(first_low, memory_low, cross_stack)
     cross_mixed, cross_logsum = attend_forward(cross_query, cross_key, cross_value, cross_allowed)
     pre_two = ALPHA * first_out + product(cross_mixed, cross_final)
     second = normalize(pre_two, gain_values[1], bias_values[1])
     second_low = rounded(second)
+
+    widen_full, narrow_full = cube.unpacked(drive.results["wide"])
 
     def widened(rows_low):
         hidden = product(rows_low, widen_full)
@@ -543,16 +595,17 @@
             ]
         )
     )
+    drive.advance(STEPS["pre"])
     drive.add(
         "S1",
         cube.scatter(
-            [(token_turned[0], jnp.concatenate([self_dq, self_dk], axis=1))], orders[SCATTER["S1"]]
+            [(drive.after(token_turned[0]), jnp.concatenate([self_dq, self_dk], axis=1))], orders[SCATTER["S1"]]
         ),
     )
     drive.add(
         "S2",
         cube.scatter(
-            [(token_turned[1], self_dv), (self_mixed_turned, self_branch)],
+            [(drive.after(token_turned[1]), self_dv), (self_mixed_turned, self_branch)],
             orders[SCATTER["S2"]],
             cube.columns(grad_norms, orders[SCATTER["S2"]]),
         ),

time: 436 us -> 410 us (0.940)
  waiting for transfers between devices: 137 us -> 114 us
  local copies, waits for them, and re-layouts: 70.6 us -> 49 us
  starting transfers between devices: 59.5 us -> 77.2 us
  matrix products: 83.8 us -> 77.9 us
    ppermute x54 -> x50, waiting for transfers between devices: 136 us -> 114 us  [swap(): lax.ppermute(block, axis, [(i, i ^ 1 << k) for i in range(self.sizes[axis...]
    ppermute x54 -> x50, starting transfers between devices: 59.1 us -> 77.2 us  [swap(): lax.ppermute(block, axis, [(i, i ^ 1 << k) for i in range(self.sizes[axis...]
    unnamed x336 -> x312, local copies, waits for them, and re-layouts: 38.4 us -> 24.1 us
    dot_general x48, matrix products: 69.3 us -> 63.3 us  [product(): return jnp.dot(first_side, other_side, preferred_element_type=jnp.float32)]
    concatenate x4 -> x0, local copies, waits for them, and re-layouts: 5.79 us -> none  [gather(): held = jnp.concatenate([held, (yield (held, bit))], axis=0)]
    concatenate x12 -> x13, other arithmetic: 10.1 us -> 11.9 us  [the longest x12 11.1 us: spread(): held = jnp.concatenate([held, (yield (held, bit))], axis=0)]
  transfers between devices with their start and end apart: 56 -> 52, of which waited for: 26 -> 20; matrix products, arithmetic and copies ran while one was open for 33% -> 30% of each run, Pallas kernels for 4% -> 6%
where the time goes in v3:
time: 410 us; the launch traced here: 403 us
  waiting for transfers between devices  114 us (28%)
  matrix products  77.9 us (19%)
  starting transfers between devices  77.2 us (19%)
  local copies, waits for them, and re-layouts  49 us (12%)
  other arithmetic  45.5 us (11%)
  Pallas kernels  22.4 us (5%)
  between operations  16.7 us (4%)
    ppermute x50, waiting for transfers between devices, swap(): lax.ppermute(block, axis, [(i, i ^ 1 << k) for i in range(self.sizes[axis...  114 us
    ppermute x50, starting transfers between devices, swap(): lax.ppermute(block, axis, [(i, i ^ 1 << k) for i in range(self.sizes[axis...  77.2 us
    dot_general x48, matrix products, product(): return jnp.dot(first_side, other_side, preferred_element_type=jnp.float32)  63.3 us
    unnamed x312, local copies, waits for them, and re-layouts  24.1 us
    pallas_call x4, Pallas kernels, natural(): pl.pallas_call(body, out_shape=[jax.ShapeDtypeStruct((count, rows, column...  14.9 us
    concatenate x12, other arithmetic, spread(): held = jnp.concatenate([held, (yield (held, bit))], axis=0)  11.1 us
    add x8, other arithmetic, scatter(): kept = kept[:middle] + got[:middle].astype(jnp.float32)  9.19 us
  transfers between devices with their start and end apart: 52, of which 20 were waited for; matrix products, arithmetic and copies ran while one was open for 30% of the time, Pallas kernels for 6%

profile of v3, /device:TPU:0, one launch (start us, length us, event | category | flops | bytes accessed | tf_op | source)
XLA Modules:
  0.0 403.1 jit_solution(5884709432234530215)
XLA Ops:
  10.7 4.1 %collective-permute-start = (bf16[1,144,1024]{2,1,0:T(8,128)(2,1)S(1)}, bf16[1,144,1024]{2,1,0:T(8,128)(2,1)S(1)}, u32[]{:S(2)}, u32[]{:S(2)}) collective-permute-start(bf16[1,144,1024]{2,1,0:T(8,128)(2,1)S(1)} %maximum_bitcast_fusion), channel_id=1, source_target_pairs={{0,4},{1,5},{2,6},{3,7},{4,0},{5,1},{6,2},{7,3},{8,12},{9,13},{10,... | collective-permute-start | bytes 884744 | tf_op jit(solution)/shard_map/ppermute | solution.py:149
  14.8 14.3 %collective-permute-done = bf16[1,144,1024]{2,1,0:T(8,128)(2,1)S(1)} collective-permute-done((bf16[1,144,1024]{2,1,0:T(8,128)(2,1)S(1)}, bf16[1,144,1024]{2,1,0:T(8,128)(2,1)S(1)}, u32[]{:S(2)}, u32[]{:S(2)}) %collective-permute-start) | collective-permute-done | bytes 294944 | tf_op jit(solution)/shard_map/ppermute | solution.py:149
  31.0 3.5 collective-permute-start.4
  38.2 11.3 %collective-permute-done.1 = bf16[2,144,1024]{2,1,0:T(8,128)(2,1)S(1)} collective-permute-done((bf16[2,144,1024]{2,1,0:T(8,128)(2,1)S(1)}, bf16[2,144,1024]{2,1,0:T(8,128)(2,1)S(1)}, u32[]{:S(2)}, u32[]{:S(2)}) %collective-permute-start.1) | collective-permute-done | bytes 589856 | tf_op jit(solution)/shard_map/ppermute | solution.py:149
  57.1 4.2 %collective-permute-done.5 = bf16[2,64,1024]{2,1,0:T(8,128)(2,1)S(1)} collective-permute-done((bf16[2,64,1024]{2,1,0:T(8,128)(2,1)S(1)}, bf16[2,64,1024]{2,1,0:T(8,128)(2,1)S(1)}, u32[]{:S(2)}, u32[]{:S(2)}) %collective-permute-start.5) | collective-permute-done | bytes 262176 | tf_op jit(solution)/shard_map/ppermute | solution.py:149
  64.5 5.0 %collective-permute-done.2 = bf16[4,80,1024]{2,1,0:T(8,128)(2,1)S(1)} collective-permute-done((bf16[4,80,1024]{2,1,0:T(8,128)(2,1)S(1)}, bf16[4,80,1024]{2,1,0:T(8,128)(2,1)S(1)}, u32[]{:S(2)}, u32[]{:S(2)}) %collective-permute-start.2) | collective-permute-done | bytes 655392 | tf_op jit(solution)/shard_map/ppermute | solution.py:149
  70.8 2.5 collective-permute-start.8
  74.4 20.4 %collective-permute-done.8 = bf16[8,64,1024]{2,1,0:T(8,128)(2,1)S(1)} collective-permute-done((bf16[8,64,1024]{2,1,0:T(8,128)(2,1)}, bf16[8,64,1024]{2,1,0:T(8,128)(2,1)S(1)}, u32[]{:S(2)}, u32[]{:S(2)}) %collective-permute-start.8) | collective-permute-done | bytes 1048608 | tf_op jit(solution)/shard_map/ppermute | solution.py:149
  96.4 2.8 collective-permute-done.7
  102.0 6.6 %collective-permute-done.12 = bf16[4,32,1024]{2,1,0:T(8,128)(2,1)S(1)} collective-permute-done((bf16[4,32,1024]{2,1,0:T(8,128)(2,1)}, bf16[4,32,1024]{2,1,0:T(8,128)(2,1)S(1)}, u32[]{:S(2)}, u32[]{:S(2)}) %collective-permute-start.12) | collective-permute-done | bytes 262176 | tf_op jit(solution)/shard_map/ppermute | solution.py:149
  113.3 2.8 natural_order.5
  120.5 6.3 %natural_order.4 = (bf16[32,32,1024]{2,1,0:T(8,128)(2,1)S(1)}, bf16[32,32,1024]{2,1,0:T(8,128)(2,1)S(1)}, bf16[32,16,1024]{2,1,0:T(8,128)(2,1)S(1)}) custom-call(s32[1]{0:T(128)} %bitcast.1.index_ref, bf16[16,80,1024]{2,1,0:T(8,128)(2,1)S(1)} %pad_maximum_fusion.low_ref, bf16[16,80,1024]{2,1,0:T(8,128)(2,1)} %collective-permute-done.9.high_ref), custom_call_target="tpu_custom_call" | custom-call | tf_op jit(solution)/shard_map/natural_order/pallas_call | solution.py:200
  142.5 3.6 natural_order.6
  154.6 3.1 copy-done.75
  172.8 4.0 unpacked.1
  176.8 2.7 multiply_convert_fusion.2
  186.5 8.0 %collective-permute-done.18 = bf16[256,1024]{1,0:T(8,128)(2,1)S(1)} collective-permute-done((bf16[256,1024]{1,0:T(8,128)(2,1)S(1)}, bf16[256,1024]{1,0:T(8,128)(2,1)S(1)}, u32[]{:S(2)}, u32[]{:S(2)}) %collective-permute-start.18) | collective-permute-done | bytes 524320 | tf_op jit(solution)/shard_map/ppermute | solution.py:149
  202.3 9.3 %collective-permute-done.19 = bf16[256,1024]{1,0:T(8,128)(2,1)S(1)} collective-permute-done((bf16[256,1024]{1,0:T(8,128)(2,1)S(1)}, bf16[256,1024]{1,0:T(8,128)(2,1)S(1)}, u32[]{:S(2)}, u32[]{:S(2)}) %collective-permute-start.19) | collective-permute-done | bytes 524320 | tf_op jit(solution)/shard_map/ppermute | solution.py:149
  223.0 4.0 %collective-permute-done.20 = bf16[256,1024]{1,0:T(8,128)(2,1)S(1)} collective-permute-done((bf16[256,1024]{1,0:T(8,128)(2,1)S(1)}, bf16[256,1024]{1,0:T(8,128)(2,1)S(1)}, u32[]{:S(2)}, u32[]{:S(2)}) %collective-permute-start.20) | collective-permute-done | bytes 524320 | tf_op jit(solution)/shard_map/ppermute | solution.py:149
  238.2 3.7 multiply_reduce_fusion.1
  262.6 2.6 slice_add_fusion.3
  265.2 2.8 slice_add_fusion.4
  271.9 3.4 multiply_reduce_fusion
  304.3 3.4 fusion.33
  324.8 8.9 %collective-permute-start.42 = (bf16[64,2048]{1,0:T(8,128)(2,1)S(1)}, bf16[64,2048]{1,0:T(8,128)(2,1)S(1)}, u32[]{:S(2)}, u32[]{:S(2)}) collective-permute-start(bf16[64,2048]{1,0:T(8,128)(2,1)S(1)} %fusion.73), channel_id=1, source_target_pairs={{0,4},{1,5},{2,6},{3,7},{4,0},{5,1},{6,2},{7,3},{8,12},{9,13},{10,... | collective-permute-start | bytes 786440 | tf_op jit(solution)/shard_map/ppermute | solution.py:149
  333.8 3.0 collective-permute-start.41
  337.8 10.3 %collective-permute-done.31 = bf16[256,2048]{1,0:T(8,128)(2,1)S(1)} collective-permute-done((bf16[256,2048]{1,0:T(8,128)(2,1)S(1)}, bf16[256,2048]{1,0:T(8,128)(2,1)S(1)}, u32[]{:S(2)}, u32[]{:S(2)}) %collective-permute-start.31) | collective-permute-done | bytes 1048608 | tf_op jit(solution)/shard_map/ppermute | solution.py:149
  357.3 9.0 %collective-permute-start.45 = (bf16[32,2048]{1,0:T(8,128)(2,1)S(1)}, bf16[32,2048]{1,0:T(8,128)(2,1)S(1)}, u32[]{:S(2)}, u32[]{:S(2)}) collective-permute-start(bf16[32,2048]{1,0:T(8,128)(2,1)S(1)} %fusion.90), channel_id=1, source_target_pairs={{0,4},{1,5},{2,6},{3,7},{4,0},{5,1},{6,2},{7,3},{8,12},{9,13},{10,... | collective-permute-start | bytes 393224 | tf_op jit(solution)/shard_map/ppermute | solution.py:149
  368.5 2.8 collective-permute-done.47
  375.8 2.7 collective-permute-done.44
  378.6 6.5 %collective-permute-start.49 = (bf16[32,2176]{1,0:T(8,128)(2,1)S(1)}, bf16[32,2176]{1,0:T(8,128)(2,1)S(1)}, u32[]{:S(2)}, u32[]{:S(2)}) collective-permute-start(bf16[32,2176]{1,0:T(8,128)(2,1)S(1)} %fusion.82), channel_id=1, source_target_pairs={{0,4},{1,5},{2,6},{3,7},{4,0},{5,1},{6,2},{7,3},{8,12},{9,13},{10,... | collective-permute-start | bytes 417800 | tf_op jit(solution)/shard_map/ppermute | solution.py:149
  385.1 4.7 %collective-permute-start.48 = (bf16[32,2048]{1,0:T(8,128)(2,1)S(1)}, bf16[32,2048]{1,0:T(8,128)(2,1)S(1)}, u32[]{:S(2)}, u32[]{:S(2)}) collective-permute-start(bf16[32,2048]{1,0:T(8,128)(2,1)S(1)} %fusion.87), channel_id=1, source_target_pairs={{0,4},{1,5},{2,6},{3,7},{4,0},{5,1},{6,2},{7,3},{8,12},{9,13},{10,... | collective-permute-start | bytes 393224 | tf_op jit(solution)/shard_map/ppermute | solution.py:149
  (602 shorter events, 203.9 us)
Async XLA Ops:
  7.2 143.5 %all-gather.3.cloned.1.call-start = ((), (), s32[]{:S(2)}) async-start(), calls=%async_computation | async-start | bytes 4325376 | tf_op jit(solution)/shard_map/all_gather | solution.py:451
  10.6 162.2 %all-gather.5.cloned.1.call-start = ((), (), s32[]{:S(2)}) async-start(), calls=%async_computation.1 | async-start | bytes 8912896 | tf_op jit(solution)/shard_map/all_gather | solution.py:448
  10.7 18.4 %collective-permute-start = (bf16[1,144,1024]{2,1,0:T(8,128)(2,1)S(1)}, bf16[1,144,1024]{2,1,0:T(8,128)(2,1)S(1)}, u32[]{:S(2)}, u32[]{:S(2)}) collective-permute-start(bf16[1,144,1024]{2,1,0:T(8,128)(2,1)S(1)} %maximum_bitcast_fusion), channel_id=1, source_target_pairs={{0,4},{1,5},{2,6},{3,7},{4,0},{5,1},{6,2},{7,3},{8,12},{9,13},{10,... | collective-permute-start | bytes 884744 | tf_op jit(solution)/shard_map/ppermute | solution.py:149
  29.1 20.4 %collective-permute-start.1 = (bf16[2,144,1024]{2,1,0:T(8,128)(2,1)S(1)}, bf16[2,144,1024]{2,1,0:T(8,128)(2,1)S(1)}, u32[]{:S(2)}, u32[]{:S(2)}) collective-permute-start(bf16[2,144,1024]{2,1,0:T(8,128)(2,1)S(1)} %pad_maximum_fusion.24), channel_id=1, source_target_pairs={{0,2},{1,3},{2,0},{3,1},{4,6},{5,7},{6,4},{7,5},{8,10},{9,11},{10,... | collective-permute-start | bytes 1769480 | tf_op jit(solution)/shard_map/ppermute | solution.py:149
  31.0 21.8 %collective-permute-start.4 = (bf16[1,64,1024]{2,1,0:T(8,128)(2,1)S(1)}, bf16[1,64,1024]{2,1,0:T(8,128)(2,1)S(1)}, u32[]{:S(2)}, u32[]{:S(2)}) collective-permute-start(bf16[1,64,1024]{2,1,0:T(8,128)(2,1)S(1)} %maximum_bitcast_fusion.1), channel_id=1, source_target_pairs={{0,4},{1,5},{2,6},{3,7},{4,0},{5,1},{6,2},{7,3},{8,12},{9,13},{10,... | collective-permute-start | bytes 393224 | tf_op jit(solution)/shard_map/ppermute | solution.py:149
  36.6 18.6 %collective-permute-start.6 = (bf16[32,2048]{1,0:T(8,128)(2,1)}, bf16[32,2048]{1,0:T(8,128)(2,1)}, u32[]{:S(2)}, u32[]{:S(2)}) collective-permute-start(bf16[32,2048]{1,0:T(8,128)(2,1)} %bitcast.272), channel_id=1, source_target_pairs={{0,16},{16,0},{1,17},{17,1},{2,18},{18,2},{3,19},{19,3},{4,20},{20... | collective-permute-start | bytes 393224 | tf_op jit(solution)/shard_map/ppermute | solution.py:149
  49.7 19.8 %collective-permute-start.2 = (bf16[4,80,1024]{2,1,0:T(8,128)(2,1)S(1)}, bf16[4,80,1024]{2,1,0:T(8,128)(2,1)S(1)}, u32[]{:S(2)}, u32[]{:S(2)}) collective-permute-start(bf16[4,80,1024]{2,1,0:T(8,128)(2,1)S(1)} %slice.592), channel_id=1, source_target_pairs={{0,1},{1,0},{2,3},{3,2},{4,5},{5,4},{6,7},{7,6},{8,9},{9,8},{10,11... | collective-permute-start | bytes 1966088 | tf_op jit(solution)/shard_map/ppermute | solution.py:149
  70.8 24.0 %collective-permute-start.8 = (bf16[8,64,1024]{2,1,0:T(8,128)(2,1)}, bf16[8,64,1024]{2,1,0:T(8,128)(2,1)S(1)}, u32[]{:S(2)}, u32[]{:S(2)}) collective-permute-start(bf16[8,64,1024]{2,1,0:T(8,128)(2,1)} %pad_maximum_fusion.10), channel_id=1, source_target_pairs={{0,1},{1,0},{2,3},{3,2},{4,5},{5,4},{6,7},{7,6},{8,9},{9,8},{10,11... | collective-permute-start | bytes 3145736 | tf_op jit(solution)/shard_map/ppermute | solution.py:149
  73.3 26.0 %collective-permute-start.7 = (bf16[8,80,1024]{2,1,0:T(8,128)(2,1)}, bf16[8,80,1024]{2,1,0:T(8,128)(2,1)S(1)}, u32[]{:S(2)}, u32[]{:S(2)}) collective-permute-start(bf16[8,80,1024]{2,1,0:T(8,128)(2,1)} %pad_maximum_fusion.6), channel_id=1, source_target_pairs={{0,16},{16,0},{1,17},{17,1},{2,18},{18,2},{3,19},{19,3},{4,20},{20... | collective-permute-start | bytes 3932168 | tf_op jit(solution)/shard_map/ppermute | solution.py:149
  96.4 16.9 %collective-permute-start.10 = (bf16[16,64,1024]{2,1,0:T(8,128)(2,1)}, bf16[16,64,1024]{2,1,0:T(8,128)(2,1)}, u32[]{:S(2)}, u32[]{:S(2)}) collective-permute-start(bf16[16,64,1024]{2,1,0:T(8,128)(2,1)} %pad_maximum_fusion.3.low_ref), channel_id=1, source_target_pairs={{0,8},{8,0},{1,9},{9,1},{2,10},{10,2},{3,11},{11,3},{4,12},{12,4},... | collective-permute-start | bytes 6291464 | tf_op jit(solution)/shard_map/ppermute | solution.py:149
  99.6 20.9 %collective-permute-start.9 = (bf16[16,80,1024]{2,1,0:T(8,128)(2,1)S(1)}, bf16[16,80,1024]{2,1,0:T(8,128)(2,1)}, u32[]{:S(2)}, u32[]{:S(2)}) collective-permute-start(bf16[16,80,1024]{2,1,0:T(8,128)(2,1)S(1)} %pad_maximum_fusion.low_ref), channel_id=1, source_target_pairs={{0,8},{8,0},{1,9},{9,1},{2,10},{10,2},{3,11},{11,3},{4,12},{12,4},... | collective-permute-start | bytes 7864328 | tf_op jit(solution)/shard_map/ppermute | solution.py:149
  110.5 21.1 %collective-permute-start.13 = (bf16[8,32,1024]{2,1,0:T(8,128)(2,1)}, bf16[8,32,1024]{2,1,0:T(8,128)(2,1)}, u32[]{:S(2)}, u32[]{:S(2)}) collective-permute-start(bf16[8,32,1024]{2,1,0:T(8,128)(2,1)} %pad_maximum_fusion.27), channel_id=1, source_target_pairs={{0,1},{1,0},{2,3},{3,2},{4,5},{5,4},{6,7},{7,6},{8,9},{9,8},{10,11... | collective-permute-start | bytes 1572872 | tf_op jit(solution)/shard_map/ppermute | solution.py:149
  112.8 21.4 %collective-permute-start.15 = (bf16[8,32,1024]{2,1,0:T(8,128)(2,1)}, bf16[8,32,1024]{2,1,0:T(8,128)(2,1)}, u32[]{:S(2)}, u32[]{:S(2)}) collective-permute-start(bf16[8,32,1024]{2,1,0:T(8,128)(2,1)} %pad_maximum_fusion.28), channel_id=1, source_target_pairs={{0,16},{16,0},{1,17},{17,1},{2,18},{18,2},{3,19},{19,3},{4,20},{20... | collective-permute-start | bytes 1572872 | tf_op jit(solution)/shard_map/ppermute | solution.py:149
  162.2 14.6 %collective-permute-start.17 = (bf16[256,1024]{1,0:T(8,128)(2,1)S(1)}, bf16[256,1024]{1,0:T(8,128)(2,1)}, u32[]{:S(2)}, u32[]{:S(2)}) collective-permute-start(bf16[256,1024]{1,0:T(8,128)(2,1)S(1)} %fusion.65.refs_0_), channel_id=1, source_target_pairs={{0,16},{16,0},{1,17},{17,1},{2,18},{18,2},{3,19},{19,3},{4,20},{20... | collective-permute-start | bytes 1572872 | tf_op jit(solution)/shard_map/ppermute | solution.py:149
  232.5 32.7 %collective-permute-start.23 = (bf16[512,1024]{1,0:T(8,128)(2,1)}, bf16[512,1024]{1,0:T(8,128)(2,1)}, u32[]{:S(2)}, u32[]{:S(2)}) collective-permute-start(bf16[512,1024]{1,0:T(8,128)(2,1)} %add_convert_fusion.2), channel_id=1, source_target_pairs={{0,1},{1,0},{2,3},{3,2},{4,5},{5,4},{6,7},{7,6},{8,9},{9,8},{10,11... | collective-permute-start | bytes 3145736 | tf_op jit(solution)/shard_map/ppermute | solution.py:149
  233.3 29.3 %collective-permute-start.24 = (bf16[256,2048]{1,0:T(8,128)(2,1)}, bf16[256,2048]{1,0:T(8,128)(2,1)}, u32[]{:S(2)}, u32[]{:S(2)}) collective-permute-start(bf16[256,2048]{1,0:T(8,128)(2,1)} %add_convert_fusion.3), channel_id=1, source_target_pairs={{0,2},{1,3},{2,0},{3,1},{4,6},{5,7},{6,4},{7,5},{8,10},{9,11},{10,... | collective-permute-start | bytes 3145736 | tf_op jit(solution)/shard_map/ppermute | solution.py:149
  279.0 31.8 %collective-permute-start.28 = (bf16[256,2048]{1,0:T(8,128)(2,1)}, bf16[256,2048]{1,0:T(8,128)(2,1)}, u32[]{:S(2)}, u32[]{:S(2)}) collective-permute-start(bf16[256,2048]{1,0:T(8,128)(2,1)} %add_convert_fusion.1), channel_id=1, source_target_pairs={{0,16},{16,0},{1,17},{17,1},{2,18},{18,2},{3,19},{19,3},{4,20},{20... | collective-permute-start | bytes 3145736 | tf_op jit(solution)/shard_map/ppermute | solution.py:149
  280.5 27.2 %collective-permute-start.29 = (bf16[256,2048]{1,0:T(8,128)(2,1)}, bf16[256,2048]{1,0:T(8,128)(2,1)}, u32[]{:S(2)}, u32[]{:S(2)}) collective-permute-start(bf16[256,2048]{1,0:T(8,128)(2,1)} %pad_maximum_fusion.15), channel_id=1, source_target_pairs={{0,2},{1,3},{2,0},{3,1},{4,6},{5,7},{6,4},{7,5},{8,10},{9,11},{10,... | collective-permute-start | bytes 3145736 | tf_op jit(solution)/shard_map/ppermute | solution.py:149
  286.9 28.7 %collective-permute-start.30 = (bf16[128,2048]{1,0:T(8,128)(2,1)}, bf16[128,2048]{1,0:T(8,128)(2,1)}, u32[]{:S(2)}, u32[]{:S(2)}) collective-permute-start(bf16[128,2048]{1,0:T(8,128)(2,1)} %get-tuple-element.255), channel_id=1, source_target_pairs={{0,1},{1,0},{2,3},{3,2},{4,5},{5,4},{6,7},{7,6},{8,9},{9,8},{10,11... | collective-permute-start | bytes 1572872 | tf_op jit(solution)/shard_map/ppermute | solution.py:149
  293.7 24.9 %collective-permute-start.35 = (bf16[512,2176]{1,0:T(8,128)(2,1)}, bf16[512,2176]{1,0:T(8,128)(2,1)}, u32[]{:S(2)}, u32[]{:S(2)}) collective-permute-start(bf16[512,2176]{1,0:T(8,128)(2,1)} %pad_maximum_fusion.1), channel_id=1, source_target_pairs={{0,8},{8,0},{1,9},{9,1},{2,10},{10,2},{3,11},{11,3},{4,12},{12,4},... | collective-permute-start | bytes 6684680 | tf_op jit(solution)/shard_map/ppermute | solution.py:149
  293.7 19.7 %collective-permute-start.27 = (bf16[512,2048]{1,0:T(8,128)(2,1)}, bf16[512,2048]{1,0:T(8,128)(2,1)}, u32[]{:S(2)}, u32[]{:S(2)}) collective-permute-start(bf16[512,2048]{1,0:T(8,128)(2,1)} %convolution_convert_fusion), channel_id=1, source_target_pairs={{0,8},{8,0},{1,9},{9,1},{2,10},{10,2},{3,11},{11,3},{4,12},{12,4},... | collective-permute-start | bytes 6291464 | tf_op jit(solution)/shard_map/ppermute | solution.py:149
  307.8 17.0 %collective-permute-start.34 = (bf16[256,1024]{1,0:T(8,128)(2,1)S(1)}, bf16[256,1024]{1,0:T(8,128)(2,1)S(1)}, u32[]{:S(2)}, u32[]{:S(2)}) collective-permute-start(bf16[256,1024]{1,0:T(8,128)(2,1)S(1)} %copy-done.83), channel_id=1, source_target_pairs={{0,2},{1,3},{2,0},{3,1},{4,6},{5,7},{6,4},{7,5},{8,10},{9,11},{10,... | collective-permute-start | bytes 1572872 | tf_op jit(solution)/shard_map/ppermute | solution.py:149
  312.6 24.3 %collective-permute-start.32 = (bf16[128,2048]{1,0:T(8,128)(2,1)S(1)}, bf16[128,2048]{1,0:T(8,128)(2,1)S(1)}, u32[]{:S(2)}, u32[]{:S(2)}) collective-permute-start(bf16[128,2048]{1,0:T(8,128)(2,1)S(1)} %get-tuple-element.155), channel_id=1, source_target_pairs={{0,1},{1,0},{2,3},{3,2},{4,5},{5,4},{6,7},{7,6},{8,9},{9,8},{10,11... | collective-permute-start | bytes 1572872 | tf_op jit(solution)/shard_map/ppermute | solution.py:149
  313.4 20.4 %collective-permute-start.33 = (bf16[128,2048]{1,0:T(8,128)(2,1)S(1)}, bf16[128,2048]{1,0:T(8,128)(2,1)S(1)}, u32[]{:S(2)}, u32[]{:S(2)}) collective-permute-start(bf16[128,2048]{1,0:T(8,128)(2,1)S(1)} %get-tuple-element.156), channel_id=1, source_target_pairs={{0,16},{16,0},{1,17},{17,1},{2,18},{18,2},{3,19},{19,3},{4,20},{20... | collective-permute-start | bytes 1572872 | tf_op jit(solution)/shard_map/ppermute | solution.py:149
  315.6 32.5 %collective-permute-start.31 = (bf16[256,2048]{1,0:T(8,128)(2,1)S(1)}, bf16[256,2048]{1,0:T(8,128)(2,1)S(1)}, u32[]{:S(2)}, u32[]{:S(2)}) collective-permute-start(bf16[256,2048]{1,0:T(8,128)(2,1)S(1)} %add_convert_fusion), channel_id=1, source_target_pairs={{0,1},{1,0},{2,3},{3,2},{4,5},{5,4},{6,7},{7,6},{8,9},{9,8},{10,11... | collective-permute-start | bytes 3145736 | tf_op jit(solution)/shard_map/ppermute | solution.py:149
  322.0 28.0 %collective-permute-start.37 = (bf16[256,2176]{1,0:T(8,128)(2,1)S(1)}, bf16[256,2176]{1,0:T(8,128)(2,1)S(1)}, u32[]{:S(2)}, u32[]{:S(2)}) collective-permute-start(bf16[256,2176]{1,0:T(8,128)(2,1)S(1)} %pad_maximum_fusion.8), channel_id=1, source_target_pairs={{0,16},{16,0},{1,17},{17,1},{2,18},{18,2},{3,19},{19,3},{4,20},{20... | collective-permute-start | bytes 3342344 | tf_op jit(solution)/shard_map/ppermute | solution.py:149
  324.8 25.8 %collective-permute-start.42 = (bf16[64,2048]{1,0:T(8,128)(2,1)S(1)}, bf16[64,2048]{1,0:T(8,128)(2,1)S(1)}, u32[]{:S(2)}, u32[]{:S(2)}) collective-permute-start(bf16[64,2048]{1,0:T(8,128)(2,1)S(1)} %fusion.73), channel_id=1, source_target_pairs={{0,4},{1,5},{2,6},{3,7},{4,0},{5,1},{6,2},{7,3},{8,12},{9,13},{10,... | collective-permute-start | bytes 786440 | tf_op jit(solution)/shard_map/ppermute | solution.py:149
  333.8 21.0 %collective-permute-start.41 = (bf16[128,1024]{1,0:T(8,128)(2,1)S(1)}, bf16[128,1024]{1,0:T(8,128)(2,1)S(1)}, u32[]{:S(2)}, u32[]{:S(2)}) collective-permute-start(bf16[128,1024]{1,0:T(8,128)(2,1)S(1)} %fusion.74), channel_id=1, source_target_pairs={{0,4},{1,5},{2,6},{3,7},{4,0},{5,1},{6,2},{7,3},{8,12},{9,13},{10,... | collective-permute-start | bytes 786440 | tf_op jit(solution)/shard_map/ppermute | solution.py:149
  337.0 20.3 %collective-permute-start.39 = (bf16[64,2048]{1,0:T(8,128)(2,1)S(1)}, bf16[64,2048]{1,0:T(8,128)(2,1)S(1)}, u32[]{:S(2)}, u32[]{:S(2)}) collective-permute-start(bf16[64,2048]{1,0:T(8,128)(2,1)S(1)} %get-tuple-element.169), channel_id=1, source_target_pairs={{0,2},{1,3},{2,0},{3,1},{4,6},{5,7},{6,4},{7,5},{8,10},{9,11},{10,... | collective-permute-start | bytes 786440 | tf_op jit(solution)/shard_map/ppermute | solution.py:149
  349.9 18.5 %collective-permute-start.36 = (bf16[128,2048]{1,0:T(8,128)(2,1)S(1)}, bf16[128,2048]{1,0:T(8,128)(2,1)S(1)}, u32[]{:S(2)}, u32[]{:S(2)}) collective-permute-start(bf16[128,2048]{1,0:T(8,128)(2,1)S(1)} %get-tuple-element.165), channel_id=1, source_target_pairs={{0,16},{16,0},{1,17},{17,1},{2,18},{18,2},{3,19},{19,3},{4,20},{20... | collective-permute-start | bytes 1572872 | tf_op jit(solution)/shard_map/ppermute | solution.py:149
  350.6 17.2 %collective-permute-start.38 = (bf16[128,2176]{1,0:T(8,128)(2,1)S(1)}, bf16[128,2176]{1,0:T(8,128)(2,1)S(1)}, u32[]{:S(2)}, u32[]{:S(2)}) collective-permute-start(bf16[128,2176]{1,0:T(8,128)(2,1)S(1)} %get-tuple-element.168), channel_id=1, source_target_pairs={{0,1},{1,0},{2,3},{3,2},{4,5},{5,4},{6,7},{7,6},{8,9},{9,8},{10,11... | collective-permute-start | bytes 1671176 | tf_op jit(solution)/shard_map/ppermute | solution.py:149
  357.3 16.1 %collective-permute-start.45 = (bf16[32,2048]{1,0:T(8,128)(2,1)S(1)}, bf16[32,2048]{1,0:T(8,128)(2,1)S(1)}, u32[]{:S(2)}, u32[]{:S(2)}) collective-permute-start(bf16[32,2048]{1,0:T(8,128)(2,1)S(1)} %fusion.90), channel_id=1, source_target_pairs={{0,4},{1,5},{2,6},{3,7},{4,0},{5,1},{6,2},{7,3},{8,12},{9,13},{10,... | collective-permute-start | bytes 393224 | tf_op jit(solution)/shard_map/ppermute | solution.py:149
  (178 other events, 995.2 us)
Sparse Core Ops, SparseCore 0:
  11.6 73.5 all-gather.2
  87.5 75.3 all-gather.4
